TPU v7x, 32 devices: a whole 2x2x4 slice. The times are simulated.
32 devices in a mesh: pair: 2 (over y), row: 4 (over z), col: 4 (over x, core).
Axes of the slice: x: 2, y: 2, z: 4, core: 2. Of those that a mesh axis runs over, the one named last changes fastest.
Arguments:
- voxels: float32 [2, 15, 16, 640], P(None, None, ('pair', 'row'), 'col'), parts along dimension 2, may hold values from -6 to 6
- disparity: float32 [2, 16, 640], P(None, ('pair', 'row'), 'col'), parts along dimension 1, may hold values from 0 to 192
- hidden: bfloat16 [2, 16, 640, 128], P(None, ('pair', 'row'), 'col'), parts along dimension 1, may hold values from -1 to 1
- context: bfloat16 [2, 16, 640, 384], P(None, ('pair', 'row'), 'col'), parts along dimension 1, may hold values from -6 to 6
- embed_first: float32 [15, 256], replicated, may hold values from -1.5 to 1.5
- embed_bias: float32 [256], replicated, may hold values from -4 to 4
- embed_second: bfloat16 [256, 256], replicated, may hold values from -0.375 to 0.375
- motion_weight: float32 [36, 128], replicated, may hold values from -1 to 1
- motion_scale: float32 [128], replicated, may hold values from -4 to 4
- motion_bias: float32 [128], replicated, may hold values from -3 to 3
- gate_kernel: bfloat16 [3, 3, 256, 256], replicated, may hold values from -0.125 to 0.125
- candidate_kernel: bfloat16 [3, 3, 256, 128], replicated, may hold values from -0.125 to 0.125
- head_weight: bfloat16 [128], replicated, may hold values from -0.5 to 0.5
Outputs:
- new_hidden: bfloat16 [2, 16, 640, 128], P(None, ('pair', 'row'), 'col'), parts along dimension 1
- increment: float32 [2, 16, 640], P(None, ('pair', 'row'), 'col'), parts along dimension 1
There are 2 independent parts, one for each index of `pair`. A program takes and returns all parts, laid end to end along the dimension named above; an argument that names none is the same for every part. Nothing has to cross between parts.
All inputs are finite; a program needn't handle non-finite values.
Results may differ from a plain program's by a relative error of at most 0.0085.
Values may be sent and summed in bfloat16 or wider, within the bound.
A program may use at most 128 MiB of HBM per device.

v0:
```python
import functools

import jax
import jax.numpy as jnp
import numpy as np
from jax import lax
from jax.experimental import pallas as pl
from jax.experimental.pallas import tpu as pltpu
from jax.sharding import PartitionSpec as P

LEVELS = 4
RADIUS = 4
TAPS = 2 * RADIUS + 1
MAXDISP = 192


def pooling(length):
    table = np.zeros((length, length), np.float32)
    start = 0
    for level in range(1, LEVELS):
        group = 2**level
        for entry in range(length // group):
            table[entry * group : (entry + 1) * group, start + entry] = 1.0 / group
        start += length // group
    return jnp.asarray(table, jnp.bfloat16)


def split(values):
    high = lax.reduce_precision(values, 8, 7)
    return high.astype(jnp.bfloat16), (values - high).astype(jnp.bfloat16)


def silu_half(half):
    return half + half * jnp.tanh(half)


def dot(left, right):
    return jnp.dot(left, right, preferred_element_type=jnp.float32)


def encode_block(packed, first, second):
    stacked = jnp.concatenate([packed, packed[:16]], axis=0)
    half = lax.dot_general(stacked, first, (((0,), (0,)), ((), ())), preferred_element_type=jnp.float32)
    return dot(silu_half(half).astype(jnp.bfloat16), second).astype(jnp.bfloat16)


def lookup_plan(view, centre, width_all):
    lane = lax.broadcasted_iota(jnp.int32, (1, 128), 1)
    upper = lane >= 64
    slot = lane & 63
    level = sum((slot >= TAPS * l).astype(jnp.int32) for l in range(1, LEVELS))
    tap = slot - TAPS * level - RADIUS + upper.astype(jnp.int32)

    def by_level(values, dtype):
        out = jnp.full((1, 128), values[0], dtype)
        for l in range(1, LEVELS):
            out = jnp.where(level >= l, jnp.asarray(values[l], dtype), out)
        return out

    factor = by_level([1.0 / 2**l for l in range(LEVELS)], jnp.float32)
    length = by_level([width_all >> l for l in range(LEVELS)], jnp.int32)
    group = by_level([1 << 20, 128, 64, 32], jnp.int32)
    offset = by_level([0, width_all, width_all + 128, width_all + 192], jnp.int32)
    shrink = by_level([0, 0, 64, 96], jnp.int32)
    spot = centre * factor
    floor_value = jnp.floor(spot)
    weight = spot - floor_value
    weight = jnp.where(upper, weight, 1.0 - weight)
    index = floor_value.astype(jnp.int32) + tap
    inside = (index >= 0) & (index < length) & (slot < LEVELS * TAPS)
    weight = jnp.where(inside, weight, 0.0)
    index = jnp.minimum(jnp.maximum(index, 0), length - 1)
    if view:
        index = length - 1 - index
    block = (index >= group).astype(jnp.int32) + (index >= 2 * group).astype(jnp.int32)
    place = offset + index - block * jnp.where(level > 0, group, 0) + 256 * block
    place = place - jnp.where(block == 2, shrink, 0)
    return place, weight


def motion_of(view, query, match, disparity, position, pool, pool_last, weights, scale_bias):
    width_all = match.shape[0]
    scores = lax.dot_general(query, match, (((1,), (1,)), ((), ())), preferred_element_type=jnp.float32)
    rounded = scores.astype(jnp.bfloat16)
    pieces = [scores[:, at : at + 128] for at in range(0, width_all, 128)]
    for at in range(0, width_all - 255, 256):
        pooled = dot(rounded[:, at : at + 256], pool)
        pieces += [pooled[:, :128], pooled[:, 128:]]
    pieces.append(dot(rounded[:, width_all - 128 :], pool_last))
    place, weight = lookup_plan(view, position - disparity, width_all)
    lane = place & 127
    block = place >> 7
    taken = jnp.zeros_like(weight)
    for at, piece in enumerate(pieces):
        values = jnp.take_along_axis(piece, lane, axis=1, mode="promise_in_bounds")
        taken = jnp.where(block == at, values, taken)
    taken = taken * weight
    high = taken.astype(jnp.bfloat16)
    low = (taken - high.astype(jnp.float32)).astype(jnp.bfloat16)
    both = dot(jnp.concatenate([high, low], axis=1), weights)
    half = both[:, :128] + both[:, 128:] + disparity * scale_bias[0:1] + scale_bias[1:2]
    return silu_half(half)


def motion_kernel(packed_ref, disp_ref, first_ref, second_ref, pool_ref, last_ref, weights_ref, sb_ref, out_ref, feat):
    count, _, pixels = packed_ref.shape
    cols = pixels // 4
    me = lax.axis_index("col")
    for j in range(count):
        block = encode_block(packed_ref[j], first_ref[...], second_ref[...])
        for k in range(4):
            feat[k, j * cols : (j + 1) * cols, :] = block[k * cols : (k + 1) * cols]
    disparity = disp_ref[...].T
    own = me * cols + lax.broadcasted_iota(jnp.int32, (cols, 1), 0)
    for k in range(4):
        view = k // 2
        query = feat[k, pl.ds(pl.multiple_of(me * cols, 32), cols), :] * jnp.bfloat16(1.0 / 16)
        position = (count * cols - 1 - own if view else own).astype(jnp.float32)
        motion = motion_of(
            view, query, feat[k ^ 2], disparity[:cols, k : k + 1], position,
            pool_ref[...], last_ref[...], weights_ref[...], sb_ref[...],
        )
        out_ref[k * cols : (k + 1) * cols, :] = motion.astype(jnp.bfloat16)


def pack_inputs(voxels, disparity, embed_first, embed_bias, motion_weight, motion_scale, motion_bias):
    bins = voxels.shape[1]
    cols = voxels.shape[3]
    flat = voxels.transpose(1, 0, 2, 3).reshape(bins, -1)
    flat = jnp.concatenate([flat, jnp.ones((16 - bins, flat.shape[1]), flat.dtype)], axis=0)
    packed = jnp.concatenate(split(flat), axis=0)
    first = jnp.concatenate([embed_first, embed_bias[None]], axis=0) * 0.5
    first_high, first_low = split(first)
    first = jnp.concatenate([first_high, first_high, first_low], axis=0)
    disp = jnp.pad(disparity.reshape(4, cols), ((0, 4), (0, 256 - cols)))
    weight = jnp.pad(motion_weight * 0.5, ((0, 64 - motion_weight.shape[0]), (0, 0)))
    high, low = split(jnp.concatenate([weight, weight], axis=0))
    weights = jnp.concatenate(
        [jnp.concatenate([high, low], axis=1), jnp.concatenate([high, jnp.zeros_like(low)], axis=1)], axis=0
    )
    scale_bias = jnp.stack([motion_scale * (0.5 / MAXDISP), motion_bias * 0.5])
    return packed, disp, first, weights, scale_bias


def extended(shard, sides, width):
    for axis, dim in sides:
        size, length = (lax.axis_size(axis), shard.shape[dim])
        up = [(i, (i + 1) % size) for i in range(size - 1)]
        down = [(j, i) for i, j in up]
        last = lax.slice_in_dim(shard, length - width, length, axis=dim)
        initial = lax.slice_in_dim(shard, 0, width, axis=dim)
        before = lax.ppermute(last, axis, up)
        after = lax.ppermute(initial, axis, down)
        shard = jnp.concatenate([before, shard, after], axis=dim)
    return shard


def convolve(padded, kernel, row_count, col_count):
    windows = []
    for row_shift in range(3):
        for col_shift in range(3):
            windows.append(
                padded[:, row_shift : row_shift + row_count, col_shift : col_shift + col_count]
            )
    stacked_input = jnp.concatenate(windows, axis=-1)
    depth = 9 * kernel.shape[2]
    flat_kernel = kernel.reshape(depth, kernel.shape[-1])
    mirror_flat = kernel[:, ::-1].reshape(depth, kernel.shape[-1])
    both_kernels = jnp.stack([flat_kernel, mirror_flat])
    return jnp.einsum(
        "vyxk,vkd->vyxd", stacked_input, both_kernels, preferred_element_type=jnp.float32
    )


def local(
    voxels,
    disparity,
    hidden,
    context,
    embed_first,
    embed_bias,
    embed_second,
    motion_weight,
    motion_scale,
    motion_bias,
    gate_kernel,
    candidate_kernel,
    head_weight,
):
    row_count = hidden.shape[1]
    col_count = hidden.shape[2]
    units = hidden.shape[-1]
    packed, disp, first, weights, scale_bias = pack_inputs(
        voxels, disparity, embed_first, embed_bias, motion_weight, motion_scale, motion_bias
    )
    gathered = lax.all_gather(packed, "col", axis=0)
    count = gathered.shape[0]
    motion = pl.pallas_call(
        motion_kernel,
        out_shape=jax.ShapeDtypeStruct((4 * col_count, units), jnp.bfloat16),
        in_specs=[pl.BlockSpec(memory_space=pltpu.VMEM)] * 8,
        out_specs=pl.BlockSpec(memory_space=pltpu.VMEM),
        scratch_shapes=[pltpu.VMEM((4, count * col_count, 256), jnp.bfloat16)],
        compiler_params=pltpu.CompilerParams(vmem_limit_bytes=40 * 2**20),
    )(gathered, disp, first, embed_second, pooling(256), pooling(128), weights, scale_bias)
    motion = motion.reshape(hidden.shape)
    gate_input = jnp.concatenate([hidden, motion], axis=-1)
    gate_padded = extended(gate_input, (("row", 1), ("col", 2)), 1)
    motion_padded = gate_padded[..., units:]
    gate_terms = convolve(gate_padded, gate_kernel, row_count, col_count)
    update_gate = jax.nn.sigmoid(gate_terms[..., :units] + context[..., :units].astype(jnp.float32))
    reset_gate = jax.nn.sigmoid(
        gate_terms[..., units:] + context[..., units : 2 * units].astype(jnp.float32)
    )
    reset_state = (reset_gate * hidden.astype(jnp.float32)).astype(jnp.bfloat16)
    reset_padded = extended(reset_state, (("row", 1), ("col", 2)), 1)
    candidate_padded = jnp.concatenate([reset_padded, motion_padded], axis=-1)
    candidate = jnp.tanh(
        convolve(candidate_padded, candidate_kernel, row_count, col_count)
        + context[..., 2 * units :].astype(jnp.float32)
    )
    updated = ((1.0 - update_gate) * hidden.astype(jnp.float32) + update_gate * candidate).astype(
        jnp.bfloat16
    )
    increment = jnp.dot(updated, head_weight, preferred_element_type=jnp.float32)
    return (updated, increment)


def solution(mesh):
    tile = P(None, ("pair", "row"), "col")
    in_specs = (P(None, None, ("pair", "row"), "col"),) + (tile,) * 3 + (P(),) * 9
    return jax.shard_map(local, mesh=mesh, in_specs=in_specs, out_specs=(tile, tile), check_vma=False)
```

profile of v0, /device:TPU:1, one launch (start us, length us, event | category | flops | bytes accessed | tf_op | source)
XLA Modules:
  0.0 63.1 jit_solution(2794215890765319184)
XLA Ops:
  0.6 0.0 copy-start
  0.6 0.0 copy-start.4
  0.7 0.8 %broadcast_multiply_fusion = f32[36,128]{1,0:T(8,128)S(1)} fusion(f32[36,128]{1,0:T(8,128)} %param.22), kind=kLoop, calls=%fused_computation.82 | loop fusion | flops 4608 | bytes 36864 | tf_op jit(solution)/shard_map/mul | solution.py:136
  1.5 0.8 %copy.17 = f32[15,2,2,160]{3,2,1,0:T(2,128)S(1)} copy(f32[15,2,2,160]{3,2,0,1:T(2,128)} %bitcast.47) | data formatting | bytes 76800 | tf_op jit(solution)/shard_map/transpose | solution.py:129
  2.3 0.1 reshape.13
  2.5 6.6 %all-gather = bf16[128,640]{1,0:T(8,128)(2,1)S(1)} all-gather(bf16[32,640]{1,0:T(8,128)(2,1)S(1)} %pad_maximum_fusion.7), channel_id=2, replica_groups=mesh['pair'=2,'row'=4,'col'=4] {'col'}, dimensions={0}, use_global_device_ids=true | all-gather | bytes 204800 | tf_op jit(solution)/shard_map/all_gather | solution.py:196
  9.0 0.7 %reshape.14 = f32[4,160]{1,0:T(4,128)S(1)} reshape(f32[2,2,160]{2,1,0:T(2,128)} %param.16) | data formatting | bytes 5120 | tf_op jit(solution)/shard_map/reshape | solution.py:135
  9.7 0.7 %reduce-precision_convert_fusion.2 = (bf16[16,256]{1,0:T(8,128)(2,1)S(1)}, bf16[16,256]{1,0:T(8,128)(2,1)S(1)}) fusion(f32[1,256]{1,0:T(1,128)} %bitcast.49, f32[15,256]{1,0:T(8,128)} %param.19), kind=kLoop, calls=%fused_computation.79 | loop fusion | flops 24576 | bytes 32768 | tf_op jit(solution)/shard_map/convert_element_type | solution.py:30
  10.5 0.7 %multiply_bitcast_fusion = (f32[1,128]{1,0:T(1,128)S(1)}, f32[1,128]{1,0:T(1,128)S(1)}) fusion(f32[128]{0:T(128)} %param.24, f32[128]{0:T(128)} %param.23), kind=kLoop, calls=%fused_computation.94 | loop fusion | flops 256 | bytes 2048 | tf_op jit(solution)/shard_map/stack | solution.py:141
  11.2 0.9 %copy-done.1 = bf16[256,256]{1,0:T(8,128)(2,1)S(1)} copy-done((bf16[256,256]{1,0:T(8,128)(2,1)S(1)}, bf16[256,256]{1,0:T(8,128)(2,1)}, u32[]{:S(2)}) %copy-start.1) | copy-done | bytes 131096
  12.1 0.9 %copy-done.2 = bf16[256,256]{1,0:T(8,128)(2,1)S(1)} copy-done((bf16[256,256]{1,0:T(8,128)(2,1)S(1)}, bf16[256,256]{1,0:T(8,128)(2,1)}, u32[]{:S(2)}) %copy-start.2) | copy-done | bytes 131096
  13.0 0.8 %copy-done.3 = bf16[128,128]{1,0:T(8,128)(2,1)S(1)} copy-done((bf16[128,128]{1,0:T(8,128)(2,1)S(1)}, bf16[128,128]{1,0:T(8,128)(2,1)}, u32[]{:S(2)}) %copy-start.3) | copy-done | bytes 32792
  13.8 3.7 %shard_map.158 = bf16[640,128]{1,0:T(8,128)(2,1)S(1)} custom-call(bf16[4,32,640]{2,1,0:T(8,128)(2,1)S(1)} %bitcast.42, f32[8,256]{1,0:T(8,128)S(1)} %pad.10.disp_ref, bf16[48,256]{1,0:T(8,128)(2,1)S(1)} %pad_maximum_fusion.8.first_ref, bf16[256,256]{1,0:T(8,128)(2,1)S(1)} %copy-done.1, bf16[256,256]{1,0:T(8,128)(2,1)S(1)} %copy-done.2, ...), custom_call_target="tpu_custom_call" | custom-call | tf_op jit(solution)/shard_map/pallas_call | solution.py:198
  17.4 1.0 %fusion.32 = (bf16[2,1,160,256]{3,2,1,0:T(8,128)(2,1)S(1)}, bf16[2,1,160,256]{3,2,1,0:T(8,128)(2,1)S(1)}) fusion(bf16[2,2,160,128]{3,2,1,0:T(8,128)(2,1)} %param.17, bf16[2,2,160,128]{3,2,1,0:T(8,128)(2,1)S(1)} %bitcast.35), kind=kLoop, calls=%fused_computation.64 | loop fusion | flops 655360 | bytes 655360 | tf_op jit(solution)/shard_map/concatenate | solution.py:207
  18.4 3.5 %collective-permute-start = (bf16[2,1,160,256]{3,2,1,0:T(8,128)(2,1)S(1)}, bf16[2,1,160,256]{3,2,1,0:T(8,128)(2,1)S(1)}, u32[]{:S(2)}, u32[]{:S(2)}) collective-permute-start(bf16[2,1,160,256]{3,2,1,0:T(8,128)(2,1)S(1)} %get-tuple-element.8), channel_id=1, source_target_pairs={{0,4},{4,8},{8,12},{1,5},{5,9},{9,13},{2,6},{6,10},{10,14},{3,7},{... | collective-permute-start | bytes 491528 | tf_op jit(solution)/shard_map/ppermute | solution.py:152
  21.9 1.3 %collective-permute-start.1 = (bf16[2,1,160,256]{3,2,1,0:T(8,128)(2,1)S(1)}, bf16[2,1,160,256]{3,2,1,0:T(8,128)(2,1)S(1)}, u32[]{:S(2)}, u32[]{:S(2)}) collective-permute-start(bf16[2,1,160,256]{3,2,1,0:T(8,128)(2,1)S(1)} %get-tuple-element.9), channel_id=1, source_target_pairs={{4,0},{8,4},{12,8},{5,1},{9,5},{13,9},{6,2},{10,6},{14,10},{7,3},{... | collective-permute-start | bytes 491528 | tf_op jit(solution)/shard_map/ppermute | solution.py:153
  23.2 2.1 %collective-permute-done = bf16[2,1,160,256]{3,2,1,0:T(8,128)(2,1)S(1)} collective-permute-done((bf16[2,1,160,256]{3,2,1,0:T(8,128)(2,1)S(1)}, bf16[2,1,160,256]{3,2,1,0:T(8,128)(2,1)S(1)}, u32[]{:S(2)}, u32[]{:S(2)}) %collective-permute-start) | collective-permute-done | bytes 163872 | tf_op jit(solution)/shard_map/ppermute | solution.py:152
  25.4 3.8 %collective-permute-done.1 = bf16[2,1,160,256]{3,2,1,0:T(8,128)(2,1)S(1)} collective-permute-done((bf16[2,1,160,256]{3,2,1,0:T(8,128)(2,1)S(1)}, bf16[2,1,160,256]{3,2,1,0:T(8,128)(2,1)S(1)}, u32[]{:S(2)}, u32[]{:S(2)}) %collective-permute-start.1) | collective-permute-done | bytes 163872 | tf_op jit(solution)/shard_map/ppermute | solution.py:153
  29.2 0.7 %pad_maximum_fusion.12 = (bf16[2,4,1,256]{3,2,1,0:T(2,128)(2,1)S(1)}, bf16[2,4,1,256]{3,2,1,0:T(2,128)(2,1)S(1)}) fusion(bf16[2,1,160,256]{3,2,1,0:T(8,128)(2,1)S(1)} %collective-permute-done.1, bf16[2,1,160,256]{3,2,1,0:T(8,128)(2,1)S(1)} %collective-permute-done, bf16[2,2,160,128]{3,2,1,0:T(8,128)(2,1)S(1)} %bitcast.36, bf16[2,2,160,128]{3,2,1,0:T(8,128)(2,1)} %param.17), kind=kLoop, calls=%fused_computation.86 | loop fusion | flops 32768 | bytes 663552 | tf_op jit(solution)/shard_map/slice | solution.py:150
  29.9 4.3 %collective-permute-start.2 = (bf16[2,4,1,256]{3,2,1,0:T(2,128)(2,1)S(1)}, bf16[2,4,1,256]{3,2,1,0:T(2,128)(2,1)S(1)}, u32[]{:S(2)}, u32[]{:S(2)}) collective-permute-start(bf16[2,4,1,256]{3,2,1,0:T(2,128)(2,1)S(1)} %get-tuple-element.4), channel_id=1, source_target_pairs={{0,1},{1,2},{2,3},{4,5},{5,6},{6,7},{8,9},{9,10},{10,11},{12,13},{... | collective-permute-start | bytes 12296 | tf_op jit(solution)/shard_map/ppermute | solution.py:152
  34.2 1.9 %collective-permute-start.3 = (bf16[2,4,1,256]{3,2,1,0:T(2,128)(2,1)S(1)}, bf16[2,4,1,256]{3,2,1,0:T(2,128)(2,1)S(1)}, u32[]{:S(2)}, u32[]{:S(2)}) collective-permute-start(bf16[2,4,1,256]{3,2,1,0:T(2,128)(2,1)S(1)} %get-tuple-element.5), channel_id=1, source_target_pairs={{1,0},{2,1},{3,2},{5,4},{6,5},{7,6},{9,8},{10,9},{11,10},{13,12},{... | collective-permute-start | bytes 12296 | tf_op jit(solution)/shard_map/ppermute | solution.py:153
  36.1 1.3 %rev.6 = bf16[3,3,256,256]{3,2,1,0:T(8,128)(2,1)S(1)} reverse(bf16[3,3,256,256]{3,2,1,0:T(8,128)(2,1)} %param.25), dimensions={1} | reverse | bytes 2359296 | tf_op jit(solution)/shard_map/rev | solution.py:168
  37.5 1.7 %collective-permute-done.3 = bf16[2,4,1,256]{3,2,1,0:T(2,128)(2,1)S(1)} collective-permute-done((bf16[2,4,1,256]{3,2,1,0:T(2,128)(2,1)S(1)}, bf16[2,4,1,256]{3,2,1,0:T(2,128)(2,1)S(1)}, u32[]{:S(2)}, u32[]{:S(2)}) %collective-permute-start.3) | collective-permute-done | bytes 4128 | tf_op jit(solution)/shard_map/ppermute | solution.py:153
  39.2 0.3 pad_maximum_fusion
  39.5 0.1 slice_dynamic-update-slice_fusion.13
  39.7 0.1 slice_dynamic-update-slice_fusion.11
  39.9 0.1 slice_dynamic-update-slice_fusion.9
  40.0 0.8 %copy-done.5 = bf16[3,3,256,256]{3,2,1,0:T(8,128)(2,1)S(1)} copy-done((bf16[3,3,256,256]{3,2,1,0:T(8,128)(2,1)S(1)}, bf16[3,3,256,256]{3,2,1,0:T(8,128)(2,1)}, u32[]{:S(2)}) %copy-start.5) | copy-done | bytes 1179672
  40.7 0.9 %fusion = f32[2,2,160,256]{3,2,1,0:T(8,128)S(1)} fusion(bf16[2,2,160,2304]{3,2,1,0:T(8,128)(2,1)S(1)} %slice_dynamic-update-slice_fusion.9, bf16[1,2304,256]{2,1,0:T(8,128)(2,1)S(1)} %bitcast.44, bf16[1,2304,256]{2,1,0:T(8,128)(2,1)S(1)} %bitcast.43), kind=kOutput, calls=%fused_computation.1 | convolution fusion | flops 756154368 | bytes 5963776 | tf_op jit(solution)/shard_map/vyxk,vkd->vyxd/dot_general | solution.py:170
  41.7 1.0 %fusion.20 = bf16[2,2,160,128]{3,2,1,0:T(8,128)(2,1)S(1)} fusion(bf16[2,2,160,128]{3,2,1,0:T(8,128)(2,1)S(1)} %copy-done.4, f32[2,2,160,256]{3,2,1,0:T(8,128)S(1)} %fusion, bf16[2,2,160,384]{3,2,1,0:T(8,128)(2,1)} %param.18), kind=kLoop, calls=%fused_computation.28 | loop fusion | flops 655360 | bytes 819200 | tf_op jit(solution)/shard_map/convert_element_type | solution.py:215
  42.7 3.2 %collective-permute-start.4 = (bf16[2,1,160,128]{3,2,1,0:T(8,128)(2,1)S(1)}, bf16[2,1,160,128]{3,2,1,0:T(8,128)(2,1)S(1)}, u32[]{:S(2)}, u32[]{:S(2)}) collective-permute-start(bf16[2,1,160,128]{3,2,1,0:T(8,128)(2,1)S(1)} %get-tuple-element.10), channel_id=1, source_target_pairs={{0,4},{4,8},{8,12},{1,5},{5,9},{9,13},{2,6},{6,10},{10,14},{3,7},{... | collective-permute-start | bytes 245768 | tf_op jit(solution)/shard_map/ppermute | solution.py:152
  46.0 1.3 %collective-permute-start.5 = (bf16[2,1,160,128]{3,2,1,0:T(8,128)(2,1)S(1)}, bf16[2,1,160,128]{3,2,1,0:T(8,128)(2,1)S(1)}, u32[]{:S(2)}, u32[]{:S(2)}) collective-permute-start(bf16[2,1,160,128]{3,2,1,0:T(8,128)(2,1)S(1)} %get-tuple-element.11), channel_id=1, source_target_pairs={{4,0},{8,4},{12,8},{5,1},{9,5},{13,9},{6,2},{10,6},{14,10},{7,3},{... | collective-permute-start | bytes 245768 | tf_op jit(solution)/shard_map/ppermute | solution.py:153
  47.3 0.2 collective-permute-done.4
  47.4 3.7 %collective-permute-done.5 = bf16[2,1,160,128]{3,2,1,0:T(8,128)(2,1)S(1)} collective-permute-done((bf16[2,1,160,128]{3,2,1,0:T(8,128)(2,1)S(1)}, bf16[2,1,160,128]{3,2,1,0:T(8,128)(2,1)S(1)}, u32[]{:S(2)}, u32[]{:S(2)}) %collective-permute-start.5) | collective-permute-done | bytes 81952 | tf_op jit(solution)/shard_map/ppermute | solution.py:153
  51.2 3.4 %collective-permute-start.6 = (bf16[2,4,1,128]{3,2,1,0:T(2,128)(2,1)S(1)}, bf16[2,4,1,128]{3,2,1,0:T(2,128)(2,1)S(1)}, u32[]{:S(2)}, u32[]{:S(2)}) collective-permute-start(bf16[2,4,1,128]{3,2,1,0:T(2,128)(2,1)S(1)} %get-tuple-element.6), channel_id=1, source_target_pairs={{0,1},{1,2},{2,3},{4,5},{5,6},{6,7},{8,9},{9,10},{10,11},{12,13},{... | collective-permute-start | bytes 6152 | tf_op jit(solution)/shard_map/ppermute | solution.py:152
  54.6 1.9 %collective-permute-start.7 = (bf16[2,4,1,128]{3,2,1,0:T(2,128)(2,1)S(1)}, bf16[2,4,1,128]{3,2,1,0:T(2,128)(2,1)S(1)}, u32[]{:S(2)}, u32[]{:S(2)}) collective-permute-start(bf16[2,4,1,128]{3,2,1,0:T(2,128)(2,1)S(1)} %get-tuple-element.7), channel_id=1, source_target_pairs={{1,0},{2,1},{3,2},{5,4},{6,5},{7,6},{9,8},{10,9},{11,10},{13,12},{... | collective-permute-start | bytes 6152 | tf_op jit(solution)/shard_map/ppermute | solution.py:153
  56.6 2.9 %collective-permute-done.7 = bf16[2,4,1,128]{3,2,1,0:T(2,128)(2,1)S(1)} collective-permute-done((bf16[2,4,1,128]{3,2,1,0:T(2,128)(2,1)S(1)}, bf16[2,4,1,128]{3,2,1,0:T(2,128)(2,1)S(1)}, u32[]{:S(2)}, u32[]{:S(2)}) %collective-permute-start.7) | collective-permute-done | bytes 2080 | tf_op jit(solution)/shard_map/ppermute | solution.py:153
  59.5 0.2 fusion.16
  59.7 0.1 slice_dynamic-update-slice_fusion.7
  59.8 0.1 slice_dynamic-update-slice_fusion.6
  59.9 0.1 slice_dynamic-update-slice_fusion.4
  60.0 0.1 slice_dynamic-update-slice_fusion.3
  60.1 0.1 slice_dynamic-update-slice_fusion.1
  60.2 0.1 slice_dynamic-update-slice_fusion
  60.3 2.0 %fusion.13 = bf16[2,2,160,128]{3,2,1,0:T(8,128)(2,1)S(1)} fusion(bf16[2,2,160,2304]{3,2,1,0:T(8,128)(2,1)S(1)} %slice_dynamic-update-slice_fusion, bf16[1,2304,128]{2,1,0:T(8,128)(2,1)S(1)} %bitcast.46, bf16[1,2304,128]{2,1,0:T(8,128)(2,1)S(1)} %bitcast.45, bf16[2,2,160,128]{3,2,1,0:T(8,128)(2,1)S(1)} %copy-done.4, f32[2,2,160,256]{3,2,1,0:T(8,128)S(1)} %fusion, ...), kind=kOutput, calls=%fused_computation.17 | convolution fusion | flops 379142144 | bytes 5111808 | tf_op jit(solution)/shard_map/vyxk,vkd->vyxd/dot_general | solution.py:170
  62.3 0.0 copy-start.7
  62.3 0.2 fusion.37
  62.5 0.6 copy.23
  (32 shorter events, 0.5 us)
Async XLA Ops:
  0.6 61.7 %copy-start = (bf16[128]{0:T(256)(128)(2,1)S(1)}, bf16[128]{0:T(256)(128)(2,1)}, u32[]{:S(2)}) copy-start(bf16[128]{0:T(256)(128)(2,1)} %param.27) | copy-start | bytes 772
  0.6 38.5 %copy-start.4 = (bf16[2,2,160,128]{3,2,1,0:T(8,128)(2,1)S(1)}, bf16[2,2,160,128]{3,2,1,0:T(8,128)(2,1)}, u32[]{:S(2)}) copy-start(bf16[2,2,160,128]{3,2,1,0:T(8,128)(2,1)} %param.17) | copy-start | bytes 491524
  11.2 0.9 %copy-start.1 = (bf16[256,256]{1,0:T(8,128)(2,1)S(1)}, bf16[256,256]{1,0:T(8,128)(2,1)}, u32[]{:S(2)}) copy-start(bf16[256,256]{1,0:T(8,128)(2,1)} %second_ref.1) | copy-start | bytes 393220
  12.1 0.9 %copy-start.2 = (bf16[256,256]{1,0:T(8,128)(2,1)S(1)}, bf16[256,256]{1,0:T(8,128)(2,1)}, u32[]{:S(2)}) copy-start(bf16[256,256]{1,0:T(8,128)(2,1)} %constant.5.clone.pool_ref) | copy-start | bytes 393220
  13.0 0.8 %copy-start.3 = (bf16[128,128]{1,0:T(8,128)(2,1)S(1)}, bf16[128,128]{1,0:T(8,128)(2,1)}, u32[]{:S(2)}) copy-start(bf16[128,128]{1,0:T(8,128)(2,1)} %constant.6.clone.last_ref) | copy-start | bytes 98308
  18.4 6.9 %collective-permute-start = (bf16[2,1,160,256]{3,2,1,0:T(8,128)(2,1)S(1)}, bf16[2,1,160,256]{3,2,1,0:T(8,128)(2,1)S(1)}, u32[]{:S(2)}, u32[]{:S(2)}) collective-permute-start(bf16[2,1,160,256]{3,2,1,0:T(8,128)(2,1)S(1)} %get-tuple-element.8), channel_id=1, source_target_pairs={{0,4},{4,8},{8,12},{1,5},{5,9},{9,13},{2,6},{6,10},{10,14},{3,7},{... | collective-permute-start | bytes 491528 | tf_op jit(solution)/shard_map/ppermute | solution.py:152
  21.9 7.2 %collective-permute-start.1 = (bf16[2,1,160,256]{3,2,1,0:T(8,128)(2,1)S(1)}, bf16[2,1,160,256]{3,2,1,0:T(8,128)(2,1)S(1)}, u32[]{:S(2)}, u32[]{:S(2)}) collective-permute-start(bf16[2,1,160,256]{3,2,1,0:T(8,128)(2,1)S(1)} %get-tuple-element.9), channel_id=1, source_target_pairs={{4,0},{8,4},{12,8},{5,1},{9,5},{13,9},{6,2},{10,6},{14,10},{7,3},{... | collective-permute-start | bytes 491528 | tf_op jit(solution)/shard_map/ppermute | solution.py:153
  29.9 7.6 %collective-permute-start.2 = (bf16[2,4,1,256]{3,2,1,0:T(2,128)(2,1)S(1)}, bf16[2,4,1,256]{3,2,1,0:T(2,128)(2,1)S(1)}, u32[]{:S(2)}, u32[]{:S(2)}) collective-permute-start(bf16[2,4,1,256]{3,2,1,0:T(2,128)(2,1)S(1)} %get-tuple-element.4), channel_id=1, source_target_pairs={{0,1},{1,2},{2,3},{4,5},{5,6},{6,7},{8,9},{9,10},{10,11},{12,13},{... | collective-permute-start | bytes 12296 | tf_op jit(solution)/shard_map/ppermute | solution.py:152
  34.2 5.0 %collective-permute-start.3 = (bf16[2,4,1,256]{3,2,1,0:T(2,128)(2,1)S(1)}, bf16[2,4,1,256]{3,2,1,0:T(2,128)(2,1)S(1)}, u32[]{:S(2)}, u32[]{:S(2)}) collective-permute-start(bf16[2,4,1,256]{3,2,1,0:T(2,128)(2,1)S(1)} %get-tuple-element.5), channel_id=1, source_target_pairs={{1,0},{2,1},{3,2},{5,4},{6,5},{7,6},{9,8},{10,9},{11,10},{13,12},{... | collective-permute-start | bytes 12296 | tf_op jit(solution)/shard_map/ppermute | solution.py:153
  39.5 1.3 %copy-start.5 = (bf16[3,3,256,256]{3,2,1,0:T(8,128)(2,1)S(1)}, bf16[3,3,256,256]{3,2,1,0:T(8,128)(2,1)}, u32[]{:S(2)}) copy-start(bf16[3,3,256,256]{3,2,1,0:T(8,128)(2,1)} %param.25) | copy-start | bytes 3538948
  40.7 15.8 %copy-start.6 = (bf16[3,3,256,128]{3,2,1,0:T(8,128)(2,1)S(1)}, bf16[3,3,256,128]{3,2,1,0:T(8,128)(2,1)}, u32[]{:S(2)}) copy-start(bf16[3,3,256,128]{3,2,1,0:T(8,128)(2,1)} %param.26) | copy-start | bytes 1769476
  42.7 4.7 %collective-permute-start.4 = (bf16[2,1,160,128]{3,2,1,0:T(8,128)(2,1)S(1)}, bf16[2,1,160,128]{3,2,1,0:T(8,128)(2,1)S(1)}, u32[]{:S(2)}, u32[]{:S(2)}) collective-permute-start(bf16[2,1,160,128]{3,2,1,0:T(8,128)(2,1)S(1)} %get-tuple-element.10), channel_id=1, source_target_pairs={{0,4},{4,8},{8,12},{1,5},{5,9},{9,13},{2,6},{6,10},{10,14},{3,7},{... | collective-permute-start | bytes 245768 | tf_op jit(solution)/shard_map/ppermute | solution.py:152
  46.0 5.2 %collective-permute-start.5 = (bf16[2,1,160,128]{3,2,1,0:T(8,128)(2,1)S(1)}, bf16[2,1,160,128]{3,2,1,0:T(8,128)(2,1)S(1)}, u32[]{:S(2)}, u32[]{:S(2)}) collective-permute-start(bf16[2,1,160,128]{3,2,1,0:T(8,128)(2,1)S(1)} %get-tuple-element.11), channel_id=1, source_target_pairs={{4,0},{8,4},{12,8},{5,1},{9,5},{13,9},{6,2},{10,6},{14,10},{7,3},{... | collective-permute-start | bytes 245768 | tf_op jit(solution)/shard_map/ppermute | solution.py:153
  51.2 5.4 %collective-permute-start.6 = (bf16[2,4,1,128]{3,2,1,0:T(2,128)(2,1)S(1)}, bf16[2,4,1,128]{3,2,1,0:T(2,128)(2,1)S(1)}, u32[]{:S(2)}, u32[]{:S(2)}) collective-permute-start(bf16[2,4,1,128]{3,2,1,0:T(2,128)(2,1)S(1)} %get-tuple-element.6), channel_id=1, source_target_pairs={{0,1},{1,2},{2,3},{4,5},{5,6},{6,7},{8,9},{9,10},{10,11},{12,13},{... | collective-permute-start | bytes 6152 | tf_op jit(solution)/shard_map/ppermute | solution.py:152
  54.6 4.9 %collective-permute-start.7 = (bf16[2,4,1,128]{3,2,1,0:T(2,128)(2,1)S(1)}, bf16[2,4,1,128]{3,2,1,0:T(2,128)(2,1)S(1)}, u32[]{:S(2)}, u32[]{:S(2)}) collective-permute-start(bf16[2,4,1,128]{3,2,1,0:T(2,128)(2,1)S(1)} %get-tuple-element.7), channel_id=1, source_target_pairs={{1,0},{2,1},{3,2},{5,4},{6,5},{7,6},{9,8},{10,9},{11,10},{13,12},{... | collective-permute-start | bytes 6152 | tf_op jit(solution)/shard_map/ppermute | solution.py:153
  62.3 0.8 %copy-start.7 = (bf16[2,2,160,128]{3,2,1,0:T(8,128)(2,1)}, bf16[2,2,160,128]{3,2,1,0:T(8,128)(2,1)S(1)}, u32[]{:S(2)}) copy-start(bf16[2,2,160,128]{3,2,1,0:T(8,128)(2,1)S(1)} %fusion.13) | copy-start | bytes 491524
where the time goes:
time: 63.9 us; the launch traced here: 63.1 us
  starting transfers between devices  20.8 us (33%)
  waiting for transfers between devices  14.4 us (23%)
  local copies, waits for them, and re-layouts  8 us (13%)
  blocking collectives  6.55 us (10%)
  other arithmetic  5.54 us (9%)
  Pallas kernels  3.67 us (6%)
  matrix products  3.08 us (5%)
  between operations  1.02 us (2%)
    ppermute x4, starting transfers between devices, extended(): before = lax.ppermute(last, axis, up)  14.4 us
    ppermute x4, waiting for transfers between devices, extended(): after = lax.ppermute(initial, axis, down)  12.1 us
    all_gather x1, blocking collectives, local(): gathered = lax.all_gather(packed, 'col', axis=0)  6.55 us
    ppermute x4, starting transfers between devices, extended(): after = lax.ppermute(initial, axis, down)  6.43 us
    unnamed x31, local copies, waits for them, and re-layouts  4.13 us
    pallas_call x1, Pallas kernels, local(): pl.pallas_call(motion_kernel, out_shape=jax.ShapeDtypeStruct((4 * col_cou...  3.67 us
    dot_general x2, matrix products, convolve(): jnp.einsum('vyxk,vkd->vyxd', stacked_input, both_kernels, preferred_eleme...  2.9 us
    ppermute x4, waiting for transfers between devices, extended(): before = lax.ppermute(last, axis, up)  2.28 us
  transfers between devices with their start and end apart: 8, of which 6 were waited for; matrix products, arithmetic and copies ran while one was open for 2% of the time, Pallas kernels for 0%

commit v1 on v0

v1 whole, which is shorter than its diff:
```python
import functools

import jax
import jax.numpy as jnp
from jax import lax
from jax.experimental import pallas as pl
from jax.experimental.pallas import tpu as pltpu
from jax.sharding import PartitionSpec as P

LEVELS = 4
RADIUS = 4
TAPS = 2 * RADIUS + 1
MAXDISP = 192


def pooling(length):
    row = lax.broadcasted_iota(jnp.int32, (length, length), 0)
    column = lax.broadcasted_iota(jnp.int32, (length, length), 1)
    table = jnp.zeros((length, length), jnp.float32)
    start = 0
    for level in range(1, LEVELS):
        entries = length >> level
        hit = ((row >> level) == column - start) & (column >= start) & (column < start + entries)
        table = jnp.where(hit, 1.0 / 2**level, table)
        start += entries
    return table.astype(jnp.bfloat16)


def split(values):
    high = values.astype(jnp.bfloat16)
    return high, (values - high.astype(jnp.float32)).astype(jnp.bfloat16)


def silu_half(half):
    return half + half * jnp.tanh(half)


def dot(left, right):
    return jnp.dot(left, right, preferred_element_type=jnp.float32)


def encode_block(packed, first, second):
    stacked = jnp.concatenate([packed, packed[:16]], axis=0)
    half = lax.dot_general(stacked, first, (((0,), (0,)), ((), ())), preferred_element_type=jnp.float32)
    return dot(silu_half(half).astype(jnp.bfloat16), second).astype(jnp.bfloat16)


def lookup_plan(view, centre, width_all):
    lane = lax.broadcasted_iota(jnp.int32, (1, 128), 1)
    upper = lane >= 64
    slot = lane & 63
    level = sum((slot >= TAPS * l).astype(jnp.int32) for l in range(1, LEVELS))
    tap = slot - TAPS * level - RADIUS + upper.astype(jnp.int32)

    def by_level(values, dtype):
        out = jnp.full((1, 128), values[0], dtype)
        for l in range(1, LEVELS):
            out = jnp.where(level >= l, jnp.asarray(values[l], dtype), out)
        return out

    factor = by_level([1.0 / 2**l for l in range(LEVELS)], jnp.float32)
    length = by_level([width_all >> l for l in range(LEVELS)], jnp.int32)
    group = by_level([1 << 20, 128, 64, 32], jnp.int32)
    offset = by_level([0, width_all, width_all + 128, width_all + 192], jnp.int32)
    shrink = by_level([0, 0, 64, 96], jnp.int32)
    spot = centre * factor
    floor_value = jnp.floor(spot)
    weight = spot - floor_value
    weight = jnp.where(upper, weight, 1.0 - weight)
    index = floor_value.astype(jnp.int32) + tap
    inside = (index >= 0) & (index < length) & (slot < LEVELS * TAPS)
    weight = jnp.where(inside, weight, 0.0)
    index = jnp.minimum(jnp.maximum(index, 0), length - 1)
    if view:
        index = length - 1 - index
    block = (index >= group).astype(jnp.int32) + (index >= 2 * group).astype(jnp.int32)
    place = offset + index - block * jnp.where(level > 0, group, 0) + 256 * block
    place = place - jnp.where(block == 2, shrink, 0)
    return place, weight


def motion_of(view, query, match, disparity, position, pool, pool_last, weights, scale_bias):
    width_all = match.shape[0]
    scores = lax.dot_general(query, match, (((1,), (1,)), ((), ())), preferred_element_type=jnp.float32)
    rounded = scores.astype(jnp.bfloat16)
    pieces = [scores[:, at : at + 128] for at in range(0, width_all, 128)]
    for at in range(0, width_all - 255, 256):
        pooled = dot(rounded[:, at : at + 256], pool)
        pieces += [pooled[:, :128], pooled[:, 128:]]
    pieces.append(dot(rounded[:, width_all - 128 :], pool_last))
    place, weight = lookup_plan(view, position - disparity, width_all)
    lane = place & 127
    block = place >> 7
    taken = jnp.zeros_like(weight)
    for at, piece in enumerate(pieces):
        values = jnp.take_along_axis(piece, lane, axis=1, mode="promise_in_bounds")
        taken = jnp.where(block == at, values, taken)
    taken = taken * weight
    high = taken.astype(jnp.bfloat16)
    low = (taken - high.astype(jnp.float32)).astype(jnp.bfloat16)
    both = dot(jnp.concatenate([high, low], axis=1), weights)
    half = both[:, :128] + both[:, 128:] + disparity * scale_bias[0:1] + scale_bias[1:2]
    return silu_half(half)


DIRECTIONS = ((-1, 0), (1, 0), (0, -1), (0, 1), (-1, -1), (-1, 1), (1, -1), (1, 1))
EDGE = 16


def sigmoid(values):
    return 0.5 + 0.5 * jnp.tanh(0.5 * values)


def update_kernel(
    voxels_ref, disparity_ref, hidden_ref, context_hbm, first_ref, bias_ref, second_ref, weight_ref, scale_ref,
    shift_ref, gate_hbm, cand_hbm, head_ref,
    out_ref, step_ref,
    context, gate, cand, packed, arrived, first16, feat, weight64, disp8,
    motion, reset, rows_in, sides_in, wide, update,
    local_sem, gather_send, gather_recv, halo_send, halo_recv,
):
    views, bins, row_count, cols = voxels_ref.shape
    units = hidden_ref.shape[-1]
    count, bands = lax.axis_size("col"), lax.axis_size("row")
    me, band = lax.axis_index("col"), lax.axis_index("row")

    loads = [
        pltpu.make_async_copy(source, target, local_sem.at[at])
        for at, (source, target) in enumerate(((gate_hbm, gate), (context_hbm, context), (cand_hbm, cand)))
    ]
    for load in loads:
        load.start()

    def inside(dy, dx):
        row, col = band + dy, me + dx
        return (row >= 0) & (row < bands) & (col >= 0) & (col < count)

    barrier = pltpu.get_barrier_semaphore()
    expected = jnp.int32(count - 1)
    for d in range(1, count):
        pl.semaphore_signal(
            barrier, inc=1, device_id={"row": band, "col": lax.rem(me + d, count)}, device_id_type=pl.DeviceIdType.MESH
        )
    for dy, dx in DIRECTIONS:
        if dy:
            there = inside(dy, dx)
            expected = expected + there.astype(jnp.int32)

            @pl.when(there)
            def _(dy=dy, dx=dx):
                pl.semaphore_signal(
                    barrier, inc=1, device_id={"row": band + dy, "col": me + dx}, device_id_type=pl.DeviceIdType.MESH
                )

    pieces = [voxels_ref[k // row_count, :, k % row_count, :] for k in range(views * row_count)]
    flat = jnp.concatenate([jnp.concatenate(pieces, axis=1), jnp.ones((16 - bins, 4 * cols), jnp.float32)], axis=0)
    high, low = split(flat)
    packed[...] = jnp.concatenate([high, low], axis=0)

    for side, dy in ((0, -1), (1, 1)):

        @pl.when(jnp.logical_not(inside(dy, 0)))
        def _(side=side):
            for turn in range(3):
                rows_in[turn, side] = jnp.zeros(rows_in.shape[2:], rows_in.dtype)

    for side, dx in ((0, -1), (1, 1)):
        for at, dy in ((0, -1), (1, 0), (row_count + 1, 1)):

            @pl.when(jnp.logical_not(inside(dy, dx)))
            def _(side=side, dy=dy, at=at):
                for turn in range(3):
                    for line in range(at, at + (1 if dy else row_count)):
                        for view in range(views):
                            sides_in[turn, side, view, line] = jnp.zeros((EDGE, units), jnp.bfloat16)

    pl.semaphore_wait(barrier, expected)

    gathers = [
        pltpu.make_async_remote_copy(
            src_ref=packed, dst_ref=arrived.at[s - 1], send_sem=gather_send.at[s - 1], recv_sem=gather_recv.at[s - 1],
            device_id={"row": band, "col": lax.rem(me + count - s, count)}, device_id_type=pl.DeviceIdType.MESH,
        )
        for s in range(1, count)
    ]
    for gather in gathers:
        gather.start()

    def halo(turn, source):
        copies = []
        for q, (dy, dx) in enumerate(DIRECTIONS):
            line = 0 if dy < 0 else row_count - 1
            span = pl.ds(0 if dx < 0 else cols - EDGE, EDGE)
            side = 1 if dx < 0 else 0
            if dx == 0:
                src, dst = source.at[:, line], rows_in.at[turn, 1 if dy < 0 else 0]
            elif dy == 0:
                src, dst = source.at[:, :, span], sides_in.at[turn, side, :, pl.ds(1, row_count)]
            else:
                src = source.at[:, line, span]
                dst = sides_in.at[turn, side, :, row_count + 1 if dy < 0 else 0]
            copies.append(
                pltpu.make_async_remote_copy(
                    src_ref=src, dst_ref=dst, send_sem=halo_send.at[turn, q], recv_sem=halo_recv.at[turn, q],
                    device_id={"row": band + dy, "col": me + dx}, device_id_type=pl.DeviceIdType.MESH,
                )
            )
        return copies

    def each(copies, action, sign):
        for copy, (dy, dx) in zip(copies, DIRECTIONS):
            pl.when(inside(sign * dy, sign * dx))(functools.partial(action, copy))

    def start(copy):
        copy.start()

    def wait_recv(copy):
        copy.wait_recv()

    def wait_send(copy):
        copy.wait_send()

    halos = [halo(turn, source) for turn, source in enumerate((hidden_ref, motion, reset))]
    each(halos[0], start, 1)

    first16[0:bins] = first_ref[...] * 0.5
    first16[bins : bins + 1] = bias_ref[...] * 0.5
    first_high, first_low = split(first16[...])
    first = jnp.concatenate([first_high, first_high, first_low], axis=0)
    weight64[...] = jnp.zeros_like(weight64)
    weight64[0 : LEVELS * TAPS] = weight_ref[...] * 0.5
    high, low = split(weight64[...])
    blank = jnp.zeros_like(low)
    weights = jnp.concatenate(
        [jnp.concatenate([high, low], axis=1)] * 2 + [jnp.concatenate([high, blank], axis=1)] * 2, axis=0
    )
    scale_bias = jnp.concatenate([scale_ref[...] * (0.5 / MAXDISP), shift_ref[...] * 0.5], axis=0)
    disp8[...] = jnp.zeros_like(disp8)
    for k in range(views * row_count):
        disp8[k : k + 1, 0:cols] = disparity_ref[k // row_count, k % row_count : k % row_count + 1, :]
    disparity = disp8[...].T
    pool, pool_last = pooling(256), pooling(128)

    for s in range(count):
        if s:
            gathers[s - 1].wait_recv()
        block = encode_block(arrived[s - 1] if s else packed[...], first, second_ref[...])
        spot = pl.ds(pl.multiple_of(lax.rem(me + s, count) * cols, 32), cols)
        for k in range(views * row_count):
            feat[k, spot, :] = block[k * cols : (k + 1) * cols]

    own = me * cols + lax.broadcasted_iota(jnp.int32, (cols, 1), 0)
    for k in range(views * row_count):
        view, line = k // row_count, k % row_count
        query = feat[k, pl.ds(pl.multiple_of(me * cols, 32), cols), :] * jnp.bfloat16(1.0 / 16)
        position = (count * cols - 1 - own if view else own).astype(jnp.float32)
        other = (views - 1 - view) * row_count + line
        motion[view, line] = motion_of(
            view, query, feat[other], disparity[:cols, k : k + 1], position, pool, pool_last, weights, scale_bias
        ).astype(jnp.bfloat16)
    each(halos[1], start, 1)

    slot = lax.broadcasted_iota(jnp.int32, (EDGE, units), 0)

    def widen(turn, source):
        for view in range(views):
            for line in range(row_count + 2):
                if line == 0:
                    centre = rows_in[turn, 0, view]
                elif line == row_count + 1:
                    centre = rows_in[turn, 1, view]
                else:
                    centre = source[view, line - 1]
                left = sides_in[turn, 0, view, line].astype(jnp.float32)
                right = sides_in[turn, 1, view, line].astype(jnp.float32)
                edge = jnp.where(slot == EDGE - 1, left, right)
                ring = jnp.concatenate([centre.astype(jnp.float32), edge], axis=0)
                before = pltpu.roll(ring, 1, axis=0)[:cols]
                after = pltpu.roll(ring, cols + EDGE - 1, axis=0)[:cols]
                wide[turn, view, line, :, 0:units] = before.astype(jnp.bfloat16)
                wide[turn, view, line, :, units : 2 * units] = centre
                wide[turn, view, line, :, 2 * units :] = after.astype(jnp.bfloat16)

    def convolve(turn, view, kernel, part):
        total = None
        order = (2, 1, 0) if view else (0, 1, 2)
        for a in range(3):
            window = wide[turn, view, a : a + row_count].reshape(row_count * cols, 3 * units)
            taps = jnp.concatenate([kernel[a, b, part * units : (part + 1) * units, :] for b in order], axis=0)
            term = dot(window, taps)
            total = term if total is None else total + term
        return total

    each(halos[0], wait_recv, -1)
    widen(0, hidden_ref)
    loads[0].wait()
    gate_terms = [convolve(0, view, gate, 0) for view in range(views)]
    loads[1].wait()
    each(halos[1], wait_recv, -1)
    widen(1, motion)
    for view in range(views):
        terms = gate_terms[view] + convolve(1, view, gate, 1)
        around = context[view, :, :, 0 : 2 * units].reshape(row_count * cols, 2 * units).astype(jnp.float32)
        gates = sigmoid(terms + around)
        update[view] = gates[:, :units]
        state = hidden_ref[view].reshape(row_count * cols, units).astype(jnp.float32)
        kept = (gates[:, units:] * state).astype(jnp.bfloat16)
        reset[view] = kept.reshape(row_count, cols, units)
    each(halos[2], start, 1)
    loads[2].wait()
    cand_terms = [convolve(1, view, cand, 1) for view in range(views)]
    each(halos[2], wait_recv, -1)
    widen(2, reset)
    for view in range(views):
        terms = cand_terms[view] + convolve(2, view, cand, 0)
        around = context[view, :, :, 2 * units :].reshape(row_count * cols, units).astype(jnp.float32)
        candidate = jnp.tanh(terms + around)
        state = hidden_ref[view].reshape(row_count * cols, units).astype(jnp.float32)
        opened = update[view]
        updated = ((1.0 - opened) * state + opened * candidate).astype(jnp.bfloat16)
        out_ref[view] = updated.reshape(row_count, cols, units)
        for line in range(row_count):
            step_ref[view, line : line + 1, :] = lax.dot_general(
                head_ref[...], updated[line * cols : (line + 1) * cols], (((1,), (1,)), ((), ())),
                preferred_element_type=jnp.float32,
            )
    for gather in gathers:
        gather.wait_send()
    for copies in halos:
        each(copies, wait_send, 1)


def local(
    voxels, disparity, hidden, context, embed_first, embed_bias, embed_second, motion_weight, motion_scale,
    motion_bias, gate_kernel, candidate_kernel, head_weight,
):
    views, bins, row_count, cols = voxels.shape
    units = hidden.shape[-1]
    channels = embed_second.shape[0]
    count = lax.axis_size("col")
    pixels = views * row_count * cols
    vmem = pl.BlockSpec(memory_space=pltpu.VMEM)
    anywhere = pl.BlockSpec(memory_space=pl.ANY)
    return pl.pallas_call(
        update_kernel,
        out_shape=(
            jax.ShapeDtypeStruct(hidden.shape, jnp.bfloat16),
            jax.ShapeDtypeStruct(disparity.shape, jnp.float32),
        ),
        in_specs=[vmem] * 3 + [anywhere] + [vmem] * 6 + [anywhere] * 2 + [vmem],
        out_specs=(vmem, vmem),
        scratch_shapes=[
            pltpu.VMEM(context.shape, jnp.bfloat16),
            pltpu.VMEM(gate_kernel.shape, jnp.bfloat16),
            pltpu.VMEM(candidate_kernel.shape, jnp.bfloat16),
            pltpu.VMEM((32, pixels), jnp.bfloat16),
            pltpu.VMEM((count - 1, 32, pixels), jnp.bfloat16),
            pltpu.VMEM((16, channels), jnp.float32),
            pltpu.VMEM((views * row_count, count * cols, channels), jnp.bfloat16),
            pltpu.VMEM((64, units), jnp.float32),
            pltpu.VMEM((8, 256), jnp.float32),
            pltpu.VMEM(hidden.shape, jnp.bfloat16),
            pltpu.VMEM(hidden.shape, jnp.bfloat16),
            pltpu.VMEM((3, 2, views, cols, units), jnp.bfloat16),
            pltpu.VMEM((3, 2, views, row_count + 2, EDGE, units), jnp.bfloat16),
            pltpu.VMEM((3, views, row_count + 2, cols, 3 * units), jnp.bfloat16),
            pltpu.VMEM((views, row_count * cols, units), jnp.float32),
            pltpu.SemaphoreType.DMA((3,)),
            pltpu.SemaphoreType.DMA((count - 1,)),
            pltpu.SemaphoreType.DMA((count - 1,)),
            pltpu.SemaphoreType.DMA((3, 8)),
            pltpu.SemaphoreType.DMA((3, 8)),
        ],
        compiler_params=pltpu.CompilerParams(
            collective_id=0, has_side_effects=True, vmem_limit_bytes=48 * 2**20
        ),
    )(
        voxels, disparity, hidden, context, embed_first, embed_bias[None], embed_second, motion_weight,
        motion_scale[None], motion_bias[None], gate_kernel, candidate_kernel, head_weight[None],
    )


def solution(mesh):
    tile = P(None, ("pair", "row"), "col")
    in_specs = (P(None, None, ("pair", "row"), "col"),) + (tile,) * 3 + (P(),) * 9
    return jax.shard_map(local, mesh=mesh, in_specs=in_specs, out_specs=(tile, tile), check_vma=False)
```

time: 63.9 us -> 36.1 us (0.56)
  the two profiles are of different devices: /device:TPU:1 before, /device:TPU:0 now
where the time goes in v1:
time: 36.1 us; the launch traced here: 35.6 us
  Pallas kernels  22.8 us (63%)
  local copies, waits for them, and re-layouts  12 us (33%)
  between operations  0.66 us (2%)
    pallas_call x1, Pallas kernels, local(): pl.pallas_call(update_kernel, out_shape=(jax.ShapeDtypeStruct(hidden.shap...  22.8 us
    unnamed x28, local copies, waits for them, and re-layouts  12 us

profile of v1, /device:TPU:0, one launch (start us, length us, event | category | flops | bytes accessed | tf_op | source)
XLA Modules:
  0.0 35.6 jit_solution(12518021147257439309)
XLA Ops:
  0.6 0.0 copy-start
  0.6 1.3 %copy-done = bf16[3,3,256,256]{3,2,1,0:T(8,128)(2,1)S(1)} copy-done((bf16[3,3,256,256]{3,2,1,0:T(8,128)(2,1)S(1)}, bf16[3,3,256,256]{3,2,1,0:T(8,128)(2,1)}, u32[]{:S(2)}) %copy-start) | copy-done | bytes 1179672
  1.9 0.0 copy-start.1
  1.9 1.1 %copy-done.1 = bf16[3,3,256,128]{3,2,1,0:T(8,128)(2,1)S(1)} copy-done((bf16[3,3,256,128]{3,2,1,0:T(8,128)(2,1)S(1)}, bf16[3,3,256,128]{3,2,1,0:T(8,128)(2,1)}, u32[]{:S(2)}) %copy-start.1) | copy-done | bytes 589848
  3.0 0.0 copy-start.2
  3.0 1.0 %copy-done.2 = bf16[2,2,160,384]{3,2,1,0:T(8,128)(2,1)S(1)} copy-done((bf16[2,2,160,384]{3,2,1,0:T(8,128)(2,1)S(1)}, bf16[2,2,160,384]{3,2,1,0:T(8,128)(2,1)}, u32[]{:S(2)}) %copy-start.2) | copy-done | bytes 491544
  4.0 0.0 copy-start.3
  4.0 0.9 %copy-done.3 = bf16[2,2,160,128]{3,2,1,0:T(8,128)(2,1)S(1)} copy-done((bf16[2,2,160,128]{3,2,1,0:T(8,128)(2,1)S(1)}, bf16[2,2,160,128]{3,2,1,0:T(8,128)(2,1)}, u32[]{:S(2)}) %copy-start.3) | copy-done | bytes 163864
  4.9 0.0 copy-start.4
  4.9 0.9 %copy-done.4 = bf16[256,256]{1,0:T(8,128)(2,1)S(1)} copy-done((bf16[256,256]{1,0:T(8,128)(2,1)S(1)}, bf16[256,256]{1,0:T(8,128)(2,1)}, u32[]{:S(2)}) %copy-start.4) | copy-done | bytes 131096
  5.8 0.0 copy-start.5
  5.8 0.8 %copy-done.5 = f32[2,15,2,160]{3,2,1,0:T(2,128)S(1)} copy-done((f32[2,15,2,160]{3,2,1,0:T(2,128)S(1)}, f32[2,15,2,160]{3,2,1,0:T(2,128)}, u32[]{:S(2)}) %copy-start.5) | copy-done | bytes 38424
  6.7 0.0 copy-start.6
  6.7 0.7 %copy-done.6 = f32[36,128]{1,0:T(8,128)S(1)} copy-done((f32[36,128]{1,0:T(8,128)S(1)}, f32[36,128]{1,0:T(8,128)}, u32[]{:S(2)}) %copy-start.6) | copy-done | bytes 18456
  7.4 0.0 copy-start.7
  7.4 0.7 %copy-done.7 = f32[15,256]{1,0:T(8,128)S(1)} copy-done((f32[15,256]{1,0:T(8,128)S(1)}, f32[15,256]{1,0:T(8,128)}, u32[]{:S(2)}) %copy-start.7) | copy-done | bytes 15384
  8.1 0.0 copy-start.8
  8.1 0.7 %copy-done.8 = f32[2,2,160]{2,1,0:T(2,128)S(1)} copy-done((f32[2,2,160]{2,1,0:T(2,128)S(1)}, f32[2,2,160]{2,1,0:T(2,128)}, u32[]{:S(2)}) %copy-start.8) | copy-done | bytes 2584
  8.8 0.0 copy-start.9
  8.8 0.7 %copy-done.9 = f32[256]{0:T(256)S(1)} copy-done((f32[256]{0:T(256)S(1)}, f32[256]{0:T(256)}, u32[]{:S(2)}) %copy-start.9) | copy-done | bytes 1048
  9.5 0.0 copy-start.10
  9.5 0.7 %copy-done.10 = f32[128]{0:T(128)S(1)} copy-done((f32[128]{0:T(128)S(1)}, f32[128]{0:T(128)}, u32[]{:S(2)}) %copy-start.10) | copy-done | bytes 536
  10.1 0.0 copy-start.11
  10.1 0.7 %copy-done.11 = f32[128]{0:T(128)S(1)} copy-done((f32[128]{0:T(128)S(1)}, f32[128]{0:T(128)}, u32[]{:S(2)}) %copy-start.11) | copy-done | bytes 536
  10.8 0.0 copy-start.12
  10.8 0.7 %copy-done.12 = bf16[128]{0:T(256)(128)(2,1)S(1)} copy-done((bf16[128]{0:T(256)(128)(2,1)S(1)}, bf16[128]{0:T(256)(128)(2,1)}, u32[]{:S(2)}) %copy-start.12) | copy-done | bytes 280
  11.4 22.8 %shard_map.140 = (bf16[2,2,160,128]{3,2,1,0:T(8,128)(2,1)S(1)}, f32[2,2,160]{2,1,0:T(2,128)S(1)}) custom-call(f32[2,15,2,160]{3,2,1,0:T(2,128)S(1)} %copy-done.5, f32[2,2,160]{2,1,0:T(2,128)S(1)} %copy-done.8, bf16[2,2,160,128]{3,2,1,0:T(8,128)(2,1)S(1)} %copy-done.3, bf16[2,2,160,384]{3,2,1,0:T(8,128)(2,1)S(1)} %copy-done.2, f32[15,256]{1,0:T(8,128)S(1)} %copy-done.7, ...), custom_call_target="tpu_custom_call" | custom-call | tf_op jit(solution)/shard_map/pallas_call | solution.py:344
  34.3 0.7 %copy.17 = bf16[2,2,160,128]{3,2,1,0:T(8,128)(2,1)} copy(bf16[2,2,160,128]{3,2,1,0:T(8,128)(2,1)S(1)} %get-tuple-element.4) | data formatting | bytes 327680
  35.0 0.6 %copy.18 = f32[2,2,160]{2,1,0:T(2,128)} copy(f32[2,2,160]{2,1,0:T(2,128)S(1)} %get-tuple-element.5) | data formatting | bytes 5120
Async XLA Ops:
  0.6 1.3 %copy-start = (bf16[3,3,256,256]{3,2,1,0:T(8,128)(2,1)S(1)}, bf16[3,3,256,256]{3,2,1,0:T(8,128)(2,1)}, u32[]{:S(2)}) copy-start(bf16[3,3,256,256]{3,2,1,0:T(8,128)(2,1)} %gate_hbm.1) | copy-start | bytes 3538948
  1.9 1.1 %copy-start.1 = (bf16[3,3,256,128]{3,2,1,0:T(8,128)(2,1)S(1)}, bf16[3,3,256,128]{3,2,1,0:T(8,128)(2,1)}, u32[]{:S(2)}) copy-start(bf16[3,3,256,128]{3,2,1,0:T(8,128)(2,1)} %cand_hbm.1) | copy-start | bytes 1769476
  3.0 1.0 %copy-start.2 = (bf16[2,2,160,384]{3,2,1,0:T(8,128)(2,1)S(1)}, bf16[2,2,160,384]{3,2,1,0:T(8,128)(2,1)}, u32[]{:S(2)}) copy-start(bf16[2,2,160,384]{3,2,1,0:T(8,128)(2,1)} %context_hbm.1) | copy-start | bytes 1474564
  4.0 0.9 %copy-start.3 = (bf16[2,2,160,128]{3,2,1,0:T(8,128)(2,1)S(1)}, bf16[2,2,160,128]{3,2,1,0:T(8,128)(2,1)}, u32[]{:S(2)}) copy-start(bf16[2,2,160,128]{3,2,1,0:T(8,128)(2,1)} %hidden_ref.1) | copy-start | bytes 491524
  4.9 0.9 %copy-start.4 = (bf16[256,256]{1,0:T(8,128)(2,1)S(1)}, bf16[256,256]{1,0:T(8,128)(2,1)}, u32[]{:S(2)}) copy-start(bf16[256,256]{1,0:T(8,128)(2,1)} %second_ref.1) | copy-start | bytes 393220
  5.8 0.8 %copy-start.5 = (f32[2,15,2,160]{3,2,1,0:T(2,128)S(1)}, f32[2,15,2,160]{3,2,1,0:T(2,128)}, u32[]{:S(2)}) copy-start(f32[2,15,2,160]{3,2,1,0:T(2,128)} %voxels_ref.1) | copy-start | bytes 115204
  6.7 0.7 %copy-start.6 = (f32[36,128]{1,0:T(8,128)S(1)}, f32[36,128]{1,0:T(8,128)}, u32[]{:S(2)}) copy-start(f32[36,128]{1,0:T(8,128)} %weight_ref.1) | copy-start | bytes 55300
  7.4 0.7 %copy-start.7 = (f32[15,256]{1,0:T(8,128)S(1)}, f32[15,256]{1,0:T(8,128)}, u32[]{:S(2)}) copy-start(f32[15,256]{1,0:T(8,128)} %first_ref.1) | copy-start | bytes 46084
  8.1 0.7 %copy-start.8 = (f32[2,2,160]{2,1,0:T(2,128)S(1)}, f32[2,2,160]{2,1,0:T(2,128)}, u32[]{:S(2)}) copy-start(f32[2,2,160]{2,1,0:T(2,128)} %disparity_ref.1) | copy-start | bytes 7684
  8.8 0.7 %copy-start.9 = (f32[256]{0:T(256)S(1)}, f32[256]{0:T(256)}, u32[]{:S(2)}) copy-start(f32[256]{0:T(256)} %param.18) | copy-start | bytes 3076
  9.5 0.7 %copy-start.10 = (f32[128]{0:T(128)S(1)}, f32[128]{0:T(128)}, u32[]{:S(2)}) copy-start(f32[128]{0:T(128)} %param.21) | copy-start | bytes 1540
  10.1 0.7 %copy-start.11 = (f32[128]{0:T(128)S(1)}, f32[128]{0:T(128)}, u32[]{:S(2)}) copy-start(f32[128]{0:T(128)} %param.22) | copy-start | bytes 1540
  10.8 0.7 %copy-start.12 = (bf16[128]{0:T(256)(128)(2,1)S(1)}, bf16[128]{0:T(256)(128)(2,1)}, u32[]{:S(2)}) copy-start(bf16[128]{0:T(256)(128)(2,1)} %param.25) | copy-start | bytes 772

commit v2 on v1

--- a/solution.py
+++ b/solution.py
@@ -112,11 +112,13 @@
 
 
 def update_kernel(
-    voxels_ref, disparity_ref, hidden_ref, context_hbm, first_ref, bias_ref, second_ref, weight_ref, scale_ref,
-    shift_ref, gate_hbm, cand_hbm, head_ref,
+    voxels_hbm, disparity_hbm, hidden_hbm, context_hbm, first_hbm, bias_hbm, second_hbm, weight_hbm, scale_hbm,
+    shift_hbm, gate_hbm, cand_hbm, head_hbm,
     out_ref, step_ref,
-    context, gate, cand, packed, arrived, first16, feat, weight64, disp8,
-    motion, reset, rows_in, sides_in, wide, update,
+    voxels_ref, disparity_ref, hidden_ref, context, first_ref, bias_ref, second_ref, weight_ref, scale_ref,
+    shift_ref, gate, cand, head_ref,
+    packed, arrived, first16, feat, weight64, disp8,
+    motion, reset, rows_in, sides_in, wide,
     local_sem, gather_send, gather_recv, halo_send, halo_recv,
 ):
     views, bins, row_count, cols = voxels_ref.shape
@@ -124,12 +126,18 @@
     count, bands = lax.axis_size("col"), lax.axis_size("row")
     me, band = lax.axis_index("col"), lax.axis_index("row")
 
-    loads = [
-        pltpu.make_async_copy(source, target, local_sem.at[at])
-        for at, (source, target) in enumerate(((gate_hbm, gate), (context_hbm, context), (cand_hbm, cand)))
-    ]
-    for load in loads:
-        load.start()
+    pairs = {
+        "voxels": (voxels_hbm, voxels_ref), "first": (first_hbm, first_ref), "bias": (bias_hbm, bias_ref),
+        "second": (second_hbm, second_ref), "weight": (weight_hbm, weight_ref), "scale": (scale_hbm, scale_ref),
+        "shift": (shift_hbm, shift_ref), "disparity": (disparity_hbm, disparity_ref),
+        "hidden": (hidden_hbm, hidden_ref), "gate": (gate_hbm, gate), "context": (context_hbm, context),
+        "cand": (cand_hbm, cand), "head": (head_hbm, head_ref),
+    }
+    loads = {
+        name: pltpu.make_async_copy(source, target, local_sem.at[at])
+        for at, (name, (source, target)) in enumerate(pairs.items())
+    }
+    loads["voxels"].start()
 
     def inside(dy, dx):
         row, col = band + dy, me + dx
@@ -152,6 +160,10 @@
                     barrier, inc=1, device_id={"row": band + dy, "col": me + dx}, device_id_type=pl.DeviceIdType.MESH
                 )
 
+    for name in list(pairs)[1:]:
+        loads[name].start()
+    loads["voxels"].wait()
+
     pieces = [voxels_ref[k // row_count, :, k % row_count, :] for k in range(views * row_count)]
     flat = jnp.concatenate([jnp.concatenate(pieces, axis=1), jnp.ones((16 - bins, 4 * cols), jnp.float32)], axis=0)
     high, low = split(flat)
@@ -186,22 +198,23 @@
     for gather in gathers:
         gather.start()
 
-    def halo(turn, source):
+    def halo(turn, view, source):
         copies = []
         for q, (dy, dx) in enumerate(DIRECTIONS):
             line = 0 if dy < 0 else row_count - 1
             span = pl.ds(0 if dx < 0 else cols - EDGE, EDGE)
             side = 1 if dx < 0 else 0
             if dx == 0:
-                src, dst = source.at[:, line], rows_in.at[turn, 1 if dy < 0 else 0]
+                src, dst = source.at[view, line], rows_in.at[turn, 1 if dy < 0 else 0, view]
             elif dy == 0:
-                src, dst = source.at[:, :, span], sides_in.at[turn, side, :, pl.ds(1, row_count)]
+                src, dst = source.at[view, :, span], sides_in.at[turn, side, view, pl.ds(1, row_count)]
             else:
-                src = source.at[:, line, span]
-                dst = sides_in.at[turn, side, :, row_count + 1 if dy < 0 else 0]
+                src = source.at[view, line, span]
+                dst = sides_in.at[turn, side, view, row_count + 1 if dy < 0 else 0]
             copies.append(
                 pltpu.make_async_remote_copy(
-                    src_ref=src, dst_ref=dst, send_sem=halo_send.at[turn, q], recv_sem=halo_recv.at[turn, q],
+                    src_ref=src, dst_ref=dst, send_sem=halo_send.at[turn, view, q],
+                    recv_sem=halo_recv.at[turn, view, q],
                     device_id={"row": band + dy, "col": me + dx}, device_id_type=pl.DeviceIdType.MESH,
                 )
             )
@@ -220,9 +233,14 @@
     def wait_send(copy):
         copy.wait_send()
 
-    halos = [halo(turn, source) for turn, source in enumerate((hidden_ref, motion, reset))]
-    each(halos[0], start, 1)
-
+    halos = [
+        [halo(turn, view, source) for view in range(views)] for turn, source in enumerate((hidden_hbm, motion, reset))
+    ]
+    for view in range(views):
+        each(halos[0][view], start, 1)
+
+    for name in ("first", "bias", "second", "weight", "scale", "shift", "disparity"):
+        loads[name].wait()
     first16[0:bins] = first_ref[...] * 0.5
     first16[bins : bins + 1] = bias_ref[...] * 0.5
     first_high, first_low = split(first16[...])
@@ -258,28 +276,28 @@
         motion[view, line] = motion_of(
             view, query, feat[other], disparity[:cols, k : k + 1], position, pool, pool_last, weights, scale_bias
         ).astype(jnp.bfloat16)
-    each(halos[1], start, 1)
+        if line == row_count - 1:
+            each(halos[1][view], start, 1)
 
     slot = lax.broadcasted_iota(jnp.int32, (EDGE, units), 0)
 
-    def widen(turn, source):
-        for view in range(views):
-            for line in range(row_count + 2):
-                if line == 0:
-                    centre = rows_in[turn, 0, view]
-                elif line == row_count + 1:
-                    centre = rows_in[turn, 1, view]
-                else:
-                    centre = source[view, line - 1]
-                left = sides_in[turn, 0, view, line].astype(jnp.float32)
-                right = sides_in[turn, 1, view, line].astype(jnp.float32)
-                edge = jnp.where(slot == EDGE - 1, left, right)
-                ring = jnp.concatenate([centre.astype(jnp.float32), edge], axis=0)
-                before = pltpu.roll(ring, 1, axis=0)[:cols]
-                after = pltpu.roll(ring, cols + EDGE - 1, axis=0)[:cols]
-                wide[turn, view, line, :, 0:units] = before.astype(jnp.bfloat16)
-                wide[turn, view, line, :, units : 2 * units] = centre
-                wide[turn, view, line, :, 2 * units :] = after.astype(jnp.bfloat16)
+    def widen(turn, view, source):
+        for line in range(row_count + 2):
+            if line == 0:
+                centre = rows_in[turn, 0, view]
+            elif line == row_count + 1:
+                centre = rows_in[turn, 1, view]
+            else:
+                centre = source[view, line - 1]
+            left = sides_in[turn, 0, view, line].astype(jnp.float32)
+            right = sides_in[turn, 1, view, line].astype(jnp.float32)
+            edge = jnp.where(slot == EDGE - 1, left, right)
+            ring = jnp.concatenate([centre.astype(jnp.float32), edge], axis=0)
+            before = pltpu.roll(ring, 1, axis=0)[:cols]
+            after = pltpu.roll(ring, cols + EDGE - 1, axis=0)[:cols]
+            wide[turn, view, line, :, 0:units] = before.astype(jnp.bfloat16)
+            wide[turn, view, line, :, units : 2 * units] = centre
+            wide[turn, view, line, :, 2 * units :] = after.astype(jnp.bfloat16)
 
     def convolve(turn, view, kernel, part):
         total = None
@@ -291,33 +309,37 @@
             total = term if total is None else total + term
         return total
 
-    each(halos[0], wait_recv, -1)
-    widen(0, hidden_ref)
-    loads[0].wait()
-    gate_terms = [convolve(0, view, gate, 0) for view in range(views)]
-    loads[1].wait()
-    each(halos[1], wait_recv, -1)
-    widen(1, motion)
+    def flat_rows(values):
+        return values.reshape(row_count * cols, values.shape[-1]).astype(jnp.float32)
+
+    loads["hidden"].wait()
+    loads["gate"].wait()
+    gate_terms = []
     for view in range(views):
+        each(halos[0][view], wait_recv, -1)
+        widen(0, view, hidden_ref)
+        gate_terms.append(convolve(0, view, gate, 0))
+    loads["context"].wait()
+    opened = []
+    for view in range(views):
+        each(halos[1][view], wait_recv, -1)
+        widen(1, view, motion)
         terms = gate_terms[view] + convolve(1, view, gate, 1)
-        around = context[view, :, :, 0 : 2 * units].reshape(row_count * cols, 2 * units).astype(jnp.float32)
-        gates = sigmoid(terms + around)
-        update[view] = gates[:, :units]
-        state = hidden_ref[view].reshape(row_count * cols, units).astype(jnp.float32)
-        kept = (gates[:, units:] * state).astype(jnp.bfloat16)
+        gates = sigmoid(terms + flat_rows(context[view, :, :, 0 : 2 * units]))
+        opened.append(gates[:, :units])
+        kept = (gates[:, units:] * flat_rows(hidden_ref[view])).astype(jnp.bfloat16)
         reset[view] = kept.reshape(row_count, cols, units)
-    each(halos[2], start, 1)
-    loads[2].wait()
+        each(halos[2][view], start, 1)
+    loads["cand"].wait()
+    loads["head"].wait()
     cand_terms = [convolve(1, view, cand, 1) for view in range(views)]
-    each(halos[2], wait_recv, -1)
-    widen(2, reset)
     for view in range(views):
+        each(halos[2][view], wait_recv, -1)
+        widen(2, view, reset)
         terms = cand_terms[view] + convolve(2, view, cand, 0)
-        around = context[view, :, :, 2 * units :].reshape(row_count * cols, units).astype(jnp.float32)
-        candidate = jnp.tanh(terms + around)
-        state = hidden_ref[view].reshape(row_count * cols, units).astype(jnp.float32)
-        opened = update[view]
-        updated = ((1.0 - opened) * state + opened * candidate).astype(jnp.bfloat16)
+        candidate = jnp.tanh(terms + flat_rows(context[view, :, :, 2 * units :]))
+        state = flat_rows(hidden_ref[view])
+        updated = ((1.0 - opened[view]) * state + opened[view] * candidate).astype(jnp.bfloat16)
         out_ref[view] = updated.reshape(row_count, cols, units)
         for line in range(row_count):
             step_ref[view, line : line + 1, :] = lax.dot_general(
@@ -326,8 +348,9 @@
             )
     for gather in gathers:
         gather.wait_send()
-    for copies in halos:
-        each(copies, wait_send, 1)
+    for turn in halos:
+        for copies in turn:
+            each(copies, wait_send, 1)
 
 
 def local(
@@ -340,19 +363,20 @@
     count = lax.axis_size("col")
     pixels = views * row_count * cols
     vmem = pl.BlockSpec(memory_space=pltpu.VMEM)
-    anywhere = pl.BlockSpec(memory_space=pl.ANY)
+    operands = (
+        voxels, disparity, hidden, context, embed_first, embed_bias[None], embed_second, motion_weight,
+        motion_scale[None], motion_bias[None], gate_kernel, candidate_kernel, head_weight[None],
+    )
     return pl.pallas_call(
         update_kernel,
         out_shape=(
             jax.ShapeDtypeStruct(hidden.shape, jnp.bfloat16),
             jax.ShapeDtypeStruct(disparity.shape, jnp.float32),
         ),
-        in_specs=[vmem] * 3 + [anywhere] + [vmem] * 6 + [anywhere] * 2 + [vmem],
+        in_specs=[pl.BlockSpec(memory_space=pltpu.HBM)] * len(operands),
         out_specs=(vmem, vmem),
-        scratch_shapes=[
-            pltpu.VMEM(context.shape, jnp.bfloat16),
-            pltpu.VMEM(gate_kernel.shape, jnp.bfloat16),
-            pltpu.VMEM(candidate_kernel.shape, jnp.bfloat16),
+        scratch_shapes=[pltpu.VMEM(operand.shape, operand.dtype) for operand in operands]
+        + [
             pltpu.VMEM((32, pixels), jnp.bfloat16),
             pltpu.VMEM((count - 1, 32, pixels), jnp.bfloat16),
             pltpu.VMEM((16, channels), jnp.float32),
@@ -364,20 +388,16 @@
             pltpu.VMEM((3, 2, views, cols, units), jnp.bfloat16),
             pltpu.VMEM((3, 2, views, row_count + 2, EDGE, units), jnp.bfloat16),
             pltpu.VMEM((3, views, row_count + 2, cols, 3 * units), jnp.bfloat16),
-            pltpu.VMEM((views, row_count * cols, units), jnp.float32),
-            pltpu.SemaphoreType.DMA((3,)),
+            pltpu.SemaphoreType.DMA((len(operands),)),
             pltpu.SemaphoreType.DMA((count - 1,)),
             pltpu.SemaphoreType.DMA((count - 1,)),
-            pltpu.SemaphoreType.DMA((3, 8)),
-            pltpu.SemaphoreType.DMA((3, 8)),
+            pltpu.SemaphoreType.DMA((3, views, 8)),
+            pltpu.SemaphoreType.DMA((3, views, 8)),
         ],
         compiler_params=pltpu.CompilerParams(
-            collective_id=0, has_side_effects=True, vmem_limit_bytes=48 * 2**20
+            collective_id=0, has_side_effects=True, vmem_limit_bytes=64 * 2**20
         ),
-    )(
-        voxels, disparity, hidden, context, embed_first, embed_bias[None], embed_second, motion_weight,
-        motion_scale[None], motion_bias[None], gate_kernel, candidate_kernel, head_weight[None],
-    )
+    )(*operands)
 
 
 def solution(mesh):

time: 36.1 us -> 25.1 us (0.70)
  local copies, waits for them, and re-layouts: 12 us -> 2.87 us
  Pallas kernels: 22.8 us -> 21.4 us
    unnamed x28 -> x2, local copies, waits for them, and re-layouts: 12 us -> 2.87 us
    pallas_call x1, Pallas kernels: 22.8 us -> 21.4 us  [local(): pl.pallas_call(update_kernel, out_shape=(jax.ShapeDtypeStruct(hidden.shap...]
where the time goes in v2:
time: 25.1 us; the launch traced here: 24.9 us
  Pallas kernels  21.4 us (85%)
  local copies, waits for them, and re-layouts  2.87 us (11%)
  between operations  0.64 us (3%)
    pallas_call x1, Pallas kernels, local(): pl.pallas_call(update_kernel, out_shape=(jax.ShapeDtypeStruct(hidden.shap...  21.4 us
    unnamed x2, local copies, waits for them, and re-layouts  2.87 us

profile of v2, /device:TPU:0, one launch (start us, length us, event | category | flops | bytes accessed | tf_op | source)
XLA Modules:
  0.0 24.9 jit_solution(513847116156526844)
XLA Ops:
  0.6 21.4 %shard_map.140 = (bf16[2,2,160,128]{3,2,1,0:T(8,128)(2,1)}, f32[2,2,160]{2,1,0:T(2,128)}) custom-call(f32[2,15,2,160]{3,2,1,0:T(2,128)} %voxels_hbm.1, f32[2,2,160]{2,1,0:T(2,128)} %disparity_hbm.1, bf16[2,2,160,128]{3,2,1,0:T(8,128)(2,1)} %hidden_hbm.1, bf16[2,2,160,384]{3,2,1,0:T(8,128)(2,1)} %context_hbm.1, f32[15,256]{1,0:T(8,128)} %first_hbm.1, ...), custom_call_target="tpu_custom_call" | custom-call | tf_op jit(solution)/shard_map/pallas_call | solution.py:370
  22.0 1.6 %copy.17 = bf16[2,2,160,128]{3,2,1,0:T(8,128)(2,1)} copy(bf16[2,2,160,128]{3,2,1,0:T(8,128)(2,1)} %get-tuple-element.4) | data formatting | bytes 327680
  23.6 1.3 %copy.18 = f32[2,2,160]{2,1,0:T(2,128)} copy(f32[2,2,160]{2,1,0:T(2,128)} %get-tuple-element.5) | data formatting | bytes 5120

commit v3 on v2

--- a/solution.py
+++ b/solution.py
@@ -114,12 +114,12 @@
 def update_kernel(
     voxels_hbm, disparity_hbm, hidden_hbm, context_hbm, first_hbm, bias_hbm, second_hbm, weight_hbm, scale_hbm,
     shift_hbm, gate_hbm, cand_hbm, head_hbm,
-    out_ref, step_ref,
+    out_hbm, step_hbm,
     voxels_ref, disparity_ref, hidden_ref, context, first_ref, bias_ref, second_ref, weight_ref, scale_ref,
     shift_ref, gate, cand, head_ref,
     packed, arrived, first16, feat, weight64, disp8,
-    motion, reset, rows_in, sides_in, wide,
-    local_sem, gather_send, gather_recv, halo_send, halo_recv,
+    motion, reset, rows_in, sides_in, wide, blank, out_ref, step_ref,
+    local_sem, out_sem, gather_send, gather_recv, halo_send, halo_recv,
 ):
     views, bins, row_count, cols = voxels_ref.shape
     units = hidden_ref.shape[-1]
@@ -169,22 +169,31 @@
     high, low = split(flat)
     packed[...] = jnp.concatenate([high, low], axis=0)
 
-    for side, dy in ((0, -1), (1, 1)):
-
-        @pl.when(jnp.logical_not(inside(dy, 0)))
-        def _(side=side):
-            for turn in range(3):
-                rows_in[turn, side] = jnp.zeros(rows_in.shape[2:], rows_in.dtype)
-
-    for side, dx in ((0, -1), (1, 1)):
-        for at, dy in ((0, -1), (1, 0), (row_count + 1, 1)):
-
-            @pl.when(jnp.logical_not(inside(dy, dx)))
-            def _(side=side, dy=dy, at=at):
-                for turn in range(3):
-                    for line in range(at, at + (1 if dy else row_count)):
-                        for view in range(views):
-                            sides_in[turn, side, view, line] = jnp.zeros((EDGE, units), jnp.bfloat16)
+    blank[...] = jnp.zeros_like(blank)
+    sources = (hidden_hbm, motion, reset)
+    parts = [(0, slice(None))] + [(turn, view) for turn in (1, 2) for view in range(views)]
+
+    def ends(turn, view, q, source):
+        dy, dx = DIRECTIONS[q]
+        line = 0 if dy < 0 else row_count - 1
+        span = pl.ds(0 if dx < 0 else cols - EDGE, EDGE)
+        side = 1 if dx < 0 else 0
+        if dx == 0:
+            return source.at[view, line], rows_in.at[turn, 1 if dy < 0 else 0, view]
+        if dy == 0:
+            return source.at[view, :, span], sides_in.at[turn, side, view, pl.ds(1, row_count)]
+        return source.at[view, line, span], sides_in.at[turn, side, view, row_count + 1 if dy < 0 else 0]
+
+    def place(turn, view):
+        return (turn, view) if turn else (0, 0)
+
+    for q, (dy, dx) in enumerate(DIRECTIONS):
+
+        @pl.when(jnp.logical_not(inside(-dy, -dx)))
+        def _(q=q):
+            for turn, view in parts:
+                src, dst = ends(turn, view, q, blank)
+                pltpu.make_async_copy(src, dst, halo_recv.at[*place(turn, view), q]).start()
 
     pl.semaphore_wait(barrier, expected)
 
@@ -198,46 +207,31 @@
     for gather in gathers:
         gather.start()
 
-    def halo(turn, view, source):
+    def halo(turn, view):
         copies = []
         for q, (dy, dx) in enumerate(DIRECTIONS):
-            line = 0 if dy < 0 else row_count - 1
-            span = pl.ds(0 if dx < 0 else cols - EDGE, EDGE)
-            side = 1 if dx < 0 else 0
-            if dx == 0:
-                src, dst = source.at[view, line], rows_in.at[turn, 1 if dy < 0 else 0, view]
-            elif dy == 0:
-                src, dst = source.at[view, :, span], sides_in.at[turn, side, view, pl.ds(1, row_count)]
-            else:
-                src = source.at[view, line, span]
-                dst = sides_in.at[turn, side, view, row_count + 1 if dy < 0 else 0]
+            src, dst = ends(turn, view, q, sources[turn])
             copies.append(
                 pltpu.make_async_remote_copy(
-                    src_ref=src, dst_ref=dst, send_sem=halo_send.at[turn, view, q],
-                    recv_sem=halo_recv.at[turn, view, q],
+                    src_ref=src, dst_ref=dst, send_sem=halo_send.at[*place(turn, view), q],
+                    recv_sem=halo_recv.at[*place(turn, view), q],
                     device_id={"row": band + dy, "col": me + dx}, device_id_type=pl.DeviceIdType.MESH,
                 )
             )
         return copies
 
-    def each(copies, action, sign):
-        for copy, (dy, dx) in zip(copies, DIRECTIONS):
-            pl.when(inside(sign * dy, sign * dx))(functools.partial(action, copy))
-
-    def start(copy):
-        copy.start()
-
-    def wait_recv(copy):
-        copy.wait_recv()
-
-    def wait_send(copy):
-        copy.wait_send()
-
-    halos = [
-        [halo(turn, view, source) for view in range(views)] for turn, source in enumerate((hidden_hbm, motion, reset))
-    ]
-    for view in range(views):
-        each(halos[0][view], start, 1)
+    halos = {part: halo(*part) for part in ((turn, 0 if turn == 0 else view) for turn, view in parts) if part[0]}
+    halos[0, 0] = halo(0, slice(None))
+
+    def start(part):
+        for copy, (dy, dx) in zip(halos[part], DIRECTIONS):
+            pl.when(inside(dy, dx))(copy.start)
+
+    def arrive(part):
+        for copy in halos[part]:
+            copy.wait_recv()
+
+    start((0, 0))
 
     for name in ("first", "bias", "second", "weight", "scale", "shift", "disparity"):
         loads[name].wait()
@@ -277,7 +271,7 @@
             view, query, feat[other], disparity[:cols, k : k + 1], position, pool, pool_last, weights, scale_bias
         ).astype(jnp.bfloat16)
         if line == row_count - 1:
-            each(halos[1][view], start, 1)
+            start((1, view))
 
     slot = lax.broadcasted_iota(jnp.int32, (EDGE, units), 0)
 
@@ -295,46 +289,52 @@
             ring = jnp.concatenate([centre.astype(jnp.float32), edge], axis=0)
             before = pltpu.roll(ring, 1, axis=0)[:cols]
             after = pltpu.roll(ring, cols + EDGE - 1, axis=0)[:cols]
+            if view:
+                before, after = after, before
             wide[turn, view, line, :, 0:units] = before.astype(jnp.bfloat16)
             wide[turn, view, line, :, units : 2 * units] = centre
             wide[turn, view, line, :, 2 * units :] = after.astype(jnp.bfloat16)
 
-    def convolve(turn, view, kernel, part):
-        total = None
-        order = (2, 1, 0) if view else (0, 1, 2)
-        for a in range(3):
-            window = wide[turn, view, a : a + row_count].reshape(row_count * cols, 3 * units)
-            taps = jnp.concatenate([kernel[a, b, part * units : (part + 1) * units, :] for b in order], axis=0)
-            term = dot(window, taps)
-            total = term if total is None else total + term
-        return total
+    def convolve(turn, first_view, kernel, part, many=1):
+        window = jnp.concatenate(
+            [
+                wide[turn, first_view : first_view + many, a : a + row_count].reshape(-1, 3 * units)
+                for a in range(3)
+            ],
+            axis=1,
+        )
+        taps = jnp.concatenate(
+            [kernel[a, b, part * units : (part + 1) * units, :] for a in range(3) for b in range(3)], axis=0
+        )
+        return dot(window, taps)
 
     def flat_rows(values):
         return values.reshape(row_count * cols, values.shape[-1]).astype(jnp.float32)
 
     loads["hidden"].wait()
     loads["gate"].wait()
-    gate_terms = []
+    arrive((0, 0))
     for view in range(views):
-        each(halos[0][view], wait_recv, -1)
         widen(0, view, hidden_ref)
-        gate_terms.append(convolve(0, view, gate, 0))
+    gate_terms = convolve(0, 0, gate, 0, views).reshape(views, row_count * cols, 2 * units)
     loads["context"].wait()
     opened = []
     for view in range(views):
-        each(halos[1][view], wait_recv, -1)
+        arrive((1, view))
         widen(1, view, motion)
         terms = gate_terms[view] + convolve(1, view, gate, 1)
         gates = sigmoid(terms + flat_rows(context[view, :, :, 0 : 2 * units]))
         opened.append(gates[:, :units])
         kept = (gates[:, units:] * flat_rows(hidden_ref[view])).astype(jnp.bfloat16)
         reset[view] = kept.reshape(row_count, cols, units)
-        each(halos[2][view], start, 1)
+        start((2, view))
     loads["cand"].wait()
     loads["head"].wait()
-    cand_terms = [convolve(1, view, cand, 1) for view in range(views)]
+    cand_terms = convolve(1, 0, cand, 1, views).reshape(views, row_count * cols, units)
+    exits = [pltpu.make_async_copy(out_ref.at[view], out_hbm.at[view], out_sem.at[view]) for view in range(views)]
+    exits.append(pltpu.make_async_copy(step_ref, step_hbm, out_sem.at[views]))
     for view in range(views):
-        each(halos[2][view], wait_recv, -1)
+        arrive((2, view))
         widen(2, view, reset)
         terms = cand_terms[view] + convolve(2, view, cand, 0)
         candidate = jnp.tanh(terms + flat_rows(context[view, :, :, 2 * units :]))
@@ -346,11 +346,30 @@
                 head_ref[...], updated[line * cols : (line + 1) * cols], (((1,), (1,)), ((), ())),
                 preferred_element_type=jnp.float32,
             )
+        exits[view].start()
+    exits[views].start()
     for gather in gathers:
         gather.wait_send()
-    for turn in halos:
-        for copies in turn:
-            each(copies, wait_send, 1)
+    for q, (dy, dx) in enumerate(DIRECTIONS):
+
+        @pl.when(inside(dy, dx))
+        def _(q=q):
+            for copies in halos.values():
+                copies[q].wait_send()
+
+    for leave in exits:
+        leave.wait()
+
+
+def hand_out(state_in, step_in, state_out, step_out, sem):
+    copies = [
+        pltpu.make_async_copy(state_in, state_out, sem.at[0]),
+        pltpu.make_async_copy(step_in, step_out, sem.at[1]),
+    ]
+    for copy in copies:
+        copy.start()
+    for copy in copies:
+        copy.wait()
 
 
 def local(
@@ -362,19 +381,20 @@
     channels = embed_second.shape[0]
     count = lax.axis_size("col")
     pixels = views * row_count * cols
-    vmem = pl.BlockSpec(memory_space=pltpu.VMEM)
+    hbm = pl.BlockSpec(memory_space=pltpu.HBM)
     operands = (
         voxels, disparity, hidden, context, embed_first, embed_bias[None], embed_second, motion_weight,
         motion_scale[None], motion_bias[None], gate_kernel, candidate_kernel, head_weight[None],
     )
-    return pl.pallas_call(
+    shapes = (
+        jax.ShapeDtypeStruct(hidden.shape, jnp.bfloat16),
+        jax.ShapeDtypeStruct(disparity.shape, jnp.float32),
+    )
+    results = pl.pallas_call(
         update_kernel,
-        out_shape=(
-            jax.ShapeDtypeStruct(hidden.shape, jnp.bfloat16),
-            jax.ShapeDtypeStruct(disparity.shape, jnp.float32),
-        ),
-        in_specs=[pl.BlockSpec(memory_space=pltpu.HBM)] * len(operands),
-        out_specs=(vmem, vmem),
+        out_shape=shapes,
+        in_specs=[hbm] * len(operands),
+        out_specs=(hbm, hbm),
         scratch_shapes=[pltpu.VMEM(operand.shape, operand.dtype) for operand in operands]
         + [
             pltpu.VMEM((32, pixels), jnp.bfloat16),
@@ -388,7 +408,11 @@
             pltpu.VMEM((3, 2, views, cols, units), jnp.bfloat16),
             pltpu.VMEM((3, 2, views, row_count + 2, EDGE, units), jnp.bfloat16),
             pltpu.VMEM((3, views, row_count + 2, cols, 3 * units), jnp.bfloat16),
+            pltpu.VMEM(hidden.shape, jnp.bfloat16),
+            pltpu.VMEM(hidden.shape, jnp.bfloat16),
+            pltpu.VMEM(disparity.shape, jnp.float32),
             pltpu.SemaphoreType.DMA((len(operands),)),
+            pltpu.SemaphoreType.DMA((views + 1,)),
             pltpu.SemaphoreType.DMA((count - 1,)),
             pltpu.SemaphoreType.DMA((count - 1,)),
             pltpu.SemaphoreType.DMA((3, views, 8)),
@@ -398,6 +422,14 @@
             collective_id=0, has_side_effects=True, vmem_limit_bytes=64 * 2**20
         ),
     )(*operands)
+    return pl.pallas_call(
+        hand_out,
+        out_shape=shapes,
+        in_specs=[hbm] * 2,
+        out_specs=(hbm, hbm),
+        scratch_shapes=[pltpu.SemaphoreType.DMA((2,))],
+        compiler_params=pltpu.CompilerParams(vmem_limit_bytes=64 * 2**20),
+    )(*results)
 
 
 def solution(mesh):

time: 25.1 us -> 28.3 us (1.13)
  Pallas kernels: 21.4 us -> 27.5 us
  local copies, waits for them, and re-layouts: 2.87 us -> 0 us
    pallas_call x1 -> x2, Pallas kernels: 21.4 us -> 27.5 us  [the longest x1 21.3 us: local(): pl.pallas_call(update_kernel, out_shape=shapes, in_specs=[hbm] * len(oper...]
    unnamed x2 -> x0, local copies, waits for them, and re-layouts: 2.87 us -> none
where the time goes in v3:
time: 28.3 us; the launch traced here: 28.2 us
  Pallas kernels  27.5 us (97%)
  between operations  0.64 us (2%)
    pallas_call x1, Pallas kernels, local(): pl.pallas_call(update_kernel, out_shape=shapes, in_specs=[hbm] * len(oper...  21.3 us
    pallas_call x1, Pallas kernels, local(): pl.pallas_call(hand_out, out_shape=shapes, in_specs=[hbm] * 2, out_specs=...  6.21 us

profile of v3, /device:TPU:0, one launch (start us, length us, event | category | flops | bytes accessed | tf_op | source)
XLA Modules:
  0.0 28.2 jit_solution(6790159427643245743)
XLA Ops:
  0.6 21.3 %shard_map.140 = (bf16[2,2,160,128]{3,2,1,0:T(8,128)(2,1)}, f32[2,2,160]{2,1,0:T(2,128)}) custom-call(f32[2,15,2,160]{3,2,1,0:T(2,128)} %voxels_hbm.1, f32[2,2,160]{2,1,0:T(2,128)} %disparity_hbm.1, bf16[2,2,160,128]{3,2,1,0:T(8,128)(2,1)} %hidden_hbm.1, bf16[2,2,160,384]{3,2,1,0:T(8,128)(2,1)} %context_hbm.1, f32[15,256]{1,0:T(8,128)} %first_hbm.1, ...), custom_call_target="tpu_custom_call" | custom-call | tf_op jit(solution)/shard_map/pallas_call | solution.py:393
  22.0 6.2 %shard_map.141 = (bf16[2,2,160,128]{3,2,1,0:T(8,128)(2,1)}, f32[2,2,160]{2,1,0:T(2,128)}) custom-call(bf16[2,2,160,128]{3,2,1,0:T(8,128)(2,1)} %get-tuple-element.4.state_in, f32[2,2,160]{2,1,0:T(2,128)} %get-tuple-element.5.step_in), custom_call_target="tpu_custom_call" | custom-call | tf_op jit(solution)/shard_map/pallas_call | solution.py:425

commit v4 on v3

--- a/solution.py
+++ b/solution.py
@@ -295,7 +295,7 @@
             wide[turn, view, line, :, units : 2 * units] = centre
             wide[turn, view, line, :, 2 * units :] = after.astype(jnp.bfloat16)
 
-    def convolve(turn, first_view, kernel, part, many=1):
+    def convolve(turn, first_view, kernel, part, channels, many=1):
         window = jnp.concatenate(
             [
                 wide[turn, first_view : first_view + many, a : a + row_count].reshape(-1, 3 * units)
@@ -304,7 +304,7 @@
             axis=1,
         )
         taps = jnp.concatenate(
-            [kernel[a, b, part * units : (part + 1) * units, :] for a in range(3) for b in range(3)], axis=0
+            [kernel[a, b, part * units : (part + 1) * units, channels] for a in range(3) for b in range(3)], axis=0
         )
         return dot(window, taps)
 
@@ -316,27 +316,28 @@
     arrive((0, 0))
     for view in range(views):
         widen(0, view, hidden_ref)
-    gate_terms = convolve(0, 0, gate, 0, views).reshape(views, row_count * cols, 2 * units)
+    early, late = slice(units, 2 * units), slice(0, units)
+    reset_terms = convolve(0, 0, gate, 0, early, views).reshape(views, row_count * cols, units)
     loads["context"].wait()
-    opened = []
     for view in range(views):
         arrive((1, view))
         widen(1, view, motion)
-        terms = gate_terms[view] + convolve(1, view, gate, 1)
-        gates = sigmoid(terms + flat_rows(context[view, :, :, 0 : 2 * units]))
-        opened.append(gates[:, :units])
-        kept = (gates[:, units:] * flat_rows(hidden_ref[view])).astype(jnp.bfloat16)
-        reset[view] = kept.reshape(row_count, cols, units)
+        terms = reset_terms[view] + convolve(1, view, gate, 1, early)
+        kept = sigmoid(terms + flat_rows(context[view, :, :, early])) * flat_rows(hidden_ref[view])
+        reset[view] = kept.astype(jnp.bfloat16).reshape(row_count, cols, units)
         start((2, view))
     loads["cand"].wait()
     loads["head"].wait()
-    cand_terms = convolve(1, 0, cand, 1, views).reshape(views, row_count * cols, units)
+    open_terms = convolve(0, 0, gate, 0, late, views) + convolve(1, 0, gate, 1, late, views)
+    opened = sigmoid(open_terms.reshape(views, row_count * cols, units) + context[:, :, :, late].reshape(
+        views, row_count * cols, units).astype(jnp.float32))
+    cand_terms = convolve(1, 0, cand, 1, late, views).reshape(views, row_count * cols, units)
     exits = [pltpu.make_async_copy(out_ref.at[view], out_hbm.at[view], out_sem.at[view]) for view in range(views)]
     exits.append(pltpu.make_async_copy(step_ref, step_hbm, out_sem.at[views]))
     for view in range(views):
         arrive((2, view))
         widen(2, view, reset)
-        terms = cand_terms[view] + convolve(2, view, cand, 0)
+        terms = cand_terms[view] + convolve(2, view, cand, 0, late)
         candidate = jnp.tanh(terms + flat_rows(context[view, :, :, 2 * units :]))
         state = flat_rows(hidden_ref[view])
         updated = ((1.0 - opened[view]) * state + opened[view] * candidate).astype(jnp.bfloat16)
@@ -361,15 +362,19 @@
         leave.wait()
 
 
-def hand_out(state_in, step_in, state_out, step_out, sem):
-    copies = [
-        pltpu.make_async_copy(state_in, state_out, sem.at[0]),
-        pltpu.make_async_copy(step_in, step_out, sem.at[1]),
-    ]
-    for copy in copies:
+def hand_out(state_in, step_in, state_out, step_out, state, step, sem):
+    views = state.shape[0]
+    arrivals = [pltpu.make_async_copy(state_in.at[view], state.at[view], sem.at[0, view]) for view in range(views)]
+    exits = [pltpu.make_async_copy(state.at[view], state_out.at[view], sem.at[1, view]) for view in range(views)]
+    arrivals.append(pltpu.make_async_copy(step_in, step, sem.at[0, views]))
+    exits.append(pltpu.make_async_copy(step, step_out, sem.at[1, views]))
+    for copy in arrivals:
         copy.start()
-    for copy in copies:
-        copy.wait()
+    for arrival, leave in zip(arrivals, exits):
+        arrival.wait()
+        leave.start()
+    for leave in exits:
+        leave.wait()
 
 
 def local(
@@ -427,7 +432,11 @@
         out_shape=shapes,
         in_specs=[hbm] * 2,
         out_specs=(hbm, hbm),
-        scratch_shapes=[pltpu.SemaphoreType.DMA((2,))],
+        scratch_shapes=[
+            pltpu.VMEM(hidden.shape, jnp.bfloat16),
+            pltpu.VMEM(disparity.shape, jnp.float32),
+            pltpu.SemaphoreType.DMA((2, views + 1)),
+        ],
         compiler_params=pltpu.CompilerParams(vmem_limit_bytes=64 * 2**20),
     )(*results)
 

time: 28.3 us -> 23.6 us (0.83)
  Pallas kernels: 27.5 us -> 22.8 us
    pallas_call x1, Pallas kernels: 6.21 us -> 1.62 us  [local(): pl.pallas_call(hand_out, out_shape=shapes, in_specs=[hbm] * 2, out_specs=...]
where the time goes in v4:
time: 23.6 us; the launch traced here: 23.4 us
  Pallas kernels  22.8 us (97%)
  between operations  0.64 us (3%)
    pallas_call x1, Pallas kernels, local(): pl.pallas_call(update_kernel, out_shape=shapes, in_specs=[hbm] * len(oper...  21.2 us
    pallas_call x1, Pallas kernels, local(): pl.pallas_call(hand_out, out_shape=shapes, in_specs=[hbm] * 2, out_specs=...  1.62 us

profile of v4, /device:TPU:0, one launch (start us, length us, event | category | flops | bytes accessed | tf_op | source)
XLA Modules:
  0.0 23.4 jit_solution(17669080024905110219)
XLA Ops:
  0.6 21.2 %shard_map.140 = (bf16[2,2,160,128]{3,2,1,0:T(8,128)(2,1)}, f32[2,2,160]{2,1,0:T(2,128)}) custom-call(f32[2,15,2,160]{3,2,1,0:T(2,128)} %voxels_hbm.1, f32[2,2,160]{2,1,0:T(2,128)} %disparity_hbm.1, bf16[2,2,160,128]{3,2,1,0:T(8,128)(2,1)} %hidden_hbm.1, bf16[2,2,160,384]{3,2,1,0:T(8,128)(2,1)} %context_hbm.1, f32[15,256]{1,0:T(8,128)} %first_hbm.1, ...), custom_call_target="tpu_custom_call" | custom-call | tf_op jit(solution)/shard_map/pallas_call | solution.py:398
  21.8 1.6 %shard_map.141 = (bf16[2,2,160,128]{3,2,1,0:T(8,128)(2,1)}, f32[2,2,160]{2,1,0:T(2,128)}) custom-call(bf16[2,2,160,128]{3,2,1,0:T(8,128)(2,1)} %get-tuple-element.4.state_in, f32[2,2,160]{2,1,0:T(2,128)} %get-tuple-element.5.step_in), custom_call_target="tpu_custom_call" | custom-call | tf_op jit(solution)/shard_map/pallas_call | solution.py:430

commit v5 on v4

--- a/solution.py
+++ b/solution.py
@@ -169,7 +169,6 @@
     high, low = split(flat)
     packed[...] = jnp.concatenate([high, low], axis=0)
 
-    blank[...] = jnp.zeros_like(blank)
     sources = (hidden_hbm, motion, reset)
     parts = [(0, slice(None))] + [(turn, view) for turn in (1, 2) for view in range(views)]
 
@@ -186,14 +185,6 @@
 
     def place(turn, view):
         return (turn, view) if turn else (0, 0)
-
-    for q, (dy, dx) in enumerate(DIRECTIONS):
-
-        @pl.when(jnp.logical_not(inside(-dy, -dx)))
-        def _(q=q):
-            for turn, view in parts:
-                src, dst = ends(turn, view, q, blank)
-                pltpu.make_async_copy(src, dst, halo_recv.at[*place(turn, view), q]).start()
 
     pl.semaphore_wait(barrier, expected)
 
@@ -223,15 +214,25 @@
     halos = {part: halo(*part) for part in ((turn, 0 if turn == 0 else view) for turn, view in parts) if part[0]}
     halos[0, 0] = halo(0, slice(None))
 
-    def start(part):
+    def start(part, ways=(-1, 0, 1)):
         for copy, (dy, dx) in zip(halos[part], DIRECTIONS):
-            pl.when(inside(dy, dx))(copy.start)
+            if dy in ways:
+                pl.when(inside(dy, dx))(copy.start)
 
     def arrive(part):
         for copy in halos[part]:
             copy.wait_recv()
 
     start((0, 0))
+
+    blank[...] = jnp.zeros_like(blank)
+    for q, (dy, dx) in enumerate(DIRECTIONS):
+
+        @pl.when(jnp.logical_not(inside(-dy, -dx)))
+        def _(q=q):
+            for turn, view in parts:
+                src, dst = ends(turn, view, q, blank)
+                pltpu.make_async_copy(src, dst, halo_recv.at[*place(turn, view), q]).start()
 
     for name in ("first", "bias", "second", "weight", "scale", "shift", "disparity"):
         loads[name].wait()
@@ -253,26 +254,6 @@
     disparity = disp8[...].T
     pool, pool_last = pooling(256), pooling(128)
 
-    for s in range(count):
-        if s:
-            gathers[s - 1].wait_recv()
-        block = encode_block(arrived[s - 1] if s else packed[...], first, second_ref[...])
-        spot = pl.ds(pl.multiple_of(lax.rem(me + s, count) * cols, 32), cols)
-        for k in range(views * row_count):
-            feat[k, spot, :] = block[k * cols : (k + 1) * cols]
-
-    own = me * cols + lax.broadcasted_iota(jnp.int32, (cols, 1), 0)
-    for k in range(views * row_count):
-        view, line = k // row_count, k % row_count
-        query = feat[k, pl.ds(pl.multiple_of(me * cols, 32), cols), :] * jnp.bfloat16(1.0 / 16)
-        position = (count * cols - 1 - own if view else own).astype(jnp.float32)
-        other = (views - 1 - view) * row_count + line
-        motion[view, line] = motion_of(
-            view, query, feat[other], disparity[:cols, k : k + 1], position, pool, pool_last, weights, scale_bias
-        ).astype(jnp.bfloat16)
-        if line == row_count - 1:
-            start((1, view))
-
     slot = lax.broadcasted_iota(jnp.int32, (EDGE, units), 0)
 
     def widen(turn, view, source):
@@ -311,25 +292,48 @@
     def flat_rows(values):
         return values.reshape(row_count * cols, values.shape[-1]).astype(jnp.float32)
 
-    loads["hidden"].wait()
-    loads["gate"].wait()
-    arrive((0, 0))
-    for view in range(views):
-        widen(0, view, hidden_ref)
-    early, late = slice(units, 2 * units), slice(0, units)
-    reset_terms = convolve(0, 0, gate, 0, early, views).reshape(views, row_count * cols, units)
+    for s in range(count):
+        if s:
+            gathers[s - 1].wait_recv()
+        block = encode_block(arrived[s - 1] if s else packed[...], first, second_ref[...])
+        spot = pl.ds(pl.multiple_of(lax.rem(me + s, count) * cols, 32), cols)
+        for k in range(views * row_count):
+            feat[k, spot, :] = block[k * cols : (k + 1) * cols]
+        if s == 0:
+            loads["hidden"].wait()
+            loads["gate"].wait()
+            arrive((0, 0))
+            for view in range(views):
+                widen(0, view, hidden_ref)
+            early, late = slice(units, 2 * units), slice(0, units)
+            gate_terms = convolve(0, 0, gate, 0, slice(0, 2 * units), views).reshape(views, row_count * cols, 2 * units)
+
+    own = me * cols + lax.broadcasted_iota(jnp.int32, (cols, 1), 0)
+    for k in range(views * row_count):
+        view, line = k // row_count, k % row_count
+        query = feat[k, pl.ds(pl.multiple_of(me * cols, 32), cols), :] * jnp.bfloat16(1.0 / 16)
+        position = (count * cols - 1 - own if view else own).astype(jnp.float32)
+        other = (views - 1 - view) * row_count + line
+        motion[view, line] = motion_of(
+            view, query, feat[other], disparity[:cols, k : k + 1], position, pool, pool_last, weights, scale_bias
+        ).astype(jnp.bfloat16)
+        if line == 0:
+            start((1, view), (-1,))
+        if line == row_count - 1:
+            start((1, view), (0, 1))
+
     loads["context"].wait()
     for view in range(views):
         arrive((1, view))
         widen(1, view, motion)
-        terms = reset_terms[view] + convolve(1, view, gate, 1, early)
+        terms = gate_terms[view][:, early] + convolve(1, view, gate, 1, early)
         kept = sigmoid(terms + flat_rows(context[view, :, :, early])) * flat_rows(hidden_ref[view])
         reset[view] = kept.astype(jnp.bfloat16).reshape(row_count, cols, units)
         start((2, view))
     loads["cand"].wait()
     loads["head"].wait()
-    open_terms = convolve(0, 0, gate, 0, late, views) + convolve(1, 0, gate, 1, late, views)
-    opened = sigmoid(open_terms.reshape(views, row_count * cols, units) + context[:, :, :, late].reshape(
+    open_terms = gate_terms[:, :, late] + convolve(1, 0, gate, 1, late, views).reshape(views, -1, units)
+    opened = sigmoid(open_terms + context[:, :, :, late].reshape(
         views, row_count * cols, units).astype(jnp.float32))
     cand_terms = convolve(1, 0, cand, 1, late, views).reshape(views, row_count * cols, units)
     exits = [pltpu.make_async_copy(out_ref.at[view], out_hbm.at[view], out_sem.at[view]) for view in range(views)]

time: 23.6 us -> 26 us (1.10)
  Pallas kernels: 22.8 us -> 25.2 us
    pallas_call x1, Pallas kernels: 21.2 us -> 23.6 us  [local(): pl.pallas_call(update_kernel, out_shape=shapes, in_specs=[hbm] * len(oper...]
where the time goes in v5:
time: 26 us; the launch traced here: 25.9 us
  Pallas kernels  25.2 us (97%)
  between operations  0.64 us (2%)
    pallas_call x1, Pallas kernels, local(): pl.pallas_call(update_kernel, out_shape=shapes, in_specs=[hbm] * len(oper...  23.6 us
    pallas_call x1, Pallas kernels, local(): pl.pallas_call(hand_out, out_shape=shapes, in_specs=[hbm] * 2, out_specs=...  1.62 us

profile of v5, /device:TPU:0, one launch (start us, length us, event | category | flops | bytes accessed | tf_op | source)
XLA Modules:
  0.0 25.9 jit_solution(2562995601357971469)
XLA Ops:
  0.6 23.6 %shard_map.140 = (bf16[2,2,160,128]{3,2,1,0:T(8,128)(2,1)}, f32[2,2,160]{2,1,0:T(2,128)}) custom-call(f32[2,15,2,160]{3,2,1,0:T(2,128)} %voxels_hbm.1, f32[2,2,160]{2,1,0:T(2,128)} %disparity_hbm.1, bf16[2,2,160,128]{3,2,1,0:T(8,128)(2,1)} %hidden_hbm.1, bf16[2,2,160,384]{3,2,1,0:T(8,128)(2,1)} %context_hbm.1, f32[15,256]{1,0:T(8,128)} %first_hbm.1, ...), custom_call_target="tpu_custom_call" | custom-call | tf_op jit(solution)/shard_map/pallas_call | solution.py:402
  24.2 1.6 %shard_map.141 = (bf16[2,2,160,128]{3,2,1,0:T(8,128)(2,1)}, f32[2,2,160]{2,1,0:T(2,128)}) custom-call(bf16[2,2,160,128]{3,2,1,0:T(8,128)(2,1)} %get-tuple-element.4.state_in, f32[2,2,160]{2,1,0:T(2,128)} %get-tuple-element.5.step_in), custom_call_target="tpu_custom_call" | custom-call | tf_op jit(solution)/shard_map/pallas_call | solution.py:434

commit v6 on v4

--- a/solution.py
+++ b/solution.py
@@ -169,7 +169,6 @@
     high, low = split(flat)
     packed[...] = jnp.concatenate([high, low], axis=0)
 
-    blank[...] = jnp.zeros_like(blank)
     sources = (hidden_hbm, motion, reset)
     parts = [(0, slice(None))] + [(turn, view) for turn in (1, 2) for view in range(views)]
 
@@ -186,14 +185,6 @@
 
     def place(turn, view):
         return (turn, view) if turn else (0, 0)
-
-    for q, (dy, dx) in enumerate(DIRECTIONS):
-
-        @pl.when(jnp.logical_not(inside(-dy, -dx)))
-        def _(q=q):
-            for turn, view in parts:
-                src, dst = ends(turn, view, q, blank)
-                pltpu.make_async_copy(src, dst, halo_recv.at[*place(turn, view), q]).start()
 
     pl.semaphore_wait(barrier, expected)
 
@@ -223,15 +214,25 @@
     halos = {part: halo(*part) for part in ((turn, 0 if turn == 0 else view) for turn, view in parts) if part[0]}
     halos[0, 0] = halo(0, slice(None))
 
-    def start(part):
+    def start(part, ways=(-1, 0, 1)):
         for copy, (dy, dx) in zip(halos[part], DIRECTIONS):
-            pl.when(inside(dy, dx))(copy.start)
+            if dy in ways:
+                pl.when(inside(dy, dx))(copy.start)
 
     def arrive(part):
         for copy in halos[part]:
             copy.wait_recv()
 
     start((0, 0))
+
+    blank[...] = jnp.zeros_like(blank)
+    for q, (dy, dx) in enumerate(DIRECTIONS):
+
+        @pl.when(jnp.logical_not(inside(-dy, -dx)))
+        def _(q=q):
+            for turn, view in parts:
+                src, dst = ends(turn, view, q, blank)
+                pltpu.make_async_copy(src, dst, halo_recv.at[*place(turn, view), q]).start()
 
     for name in ("first", "bias", "second", "weight", "scale", "shift", "disparity"):
         loads[name].wait()
@@ -270,8 +271,10 @@
         motion[view, line] = motion_of(
             view, query, feat[other], disparity[:cols, k : k + 1], position, pool, pool_last, weights, scale_bias
         ).astype(jnp.bfloat16)
+        if line == 0:
+            start((1, view), (-1,))
         if line == row_count - 1:
-            start((1, view))
+            start((1, view), (0, 1))
 
     slot = lax.broadcasted_iota(jnp.int32, (EDGE, units), 0)
 

time: 23.6 us -> 23.2 us (0.983)
  Pallas kernels: 22.8 us -> 22.3 us
    pallas_call x1, Pallas kernels: 21.2 us -> 20.7 us  [local(): pl.pallas_call(update_kernel, out_shape=shapes, in_specs=[hbm] * len(oper...]
where the time goes in v6:
time: 23.2 us; the launch traced here: 23 us
  Pallas kernels  22.3 us (96%)
  between operations  0.64 us (3%)
    pallas_call x1, Pallas kernels, local(): pl.pallas_call(update_kernel, out_shape=shapes, in_specs=[hbm] * len(oper...  20.7 us
    pallas_call x1, Pallas kernels, local(): pl.pallas_call(hand_out, out_shape=shapes, in_specs=[hbm] * 2, out_specs=...  1.62 us

profile of v6, /device:TPU:0, one launch (start us, length us, event | category | flops | bytes accessed | tf_op | source)
XLA Modules:
  0.0 23.0 jit_solution(12693548249904508266)
XLA Ops:
  0.6 20.7 %shard_map.140 = (bf16[2,2,160,128]{3,2,1,0:T(8,128)(2,1)}, f32[2,2,160]{2,1,0:T(2,128)}) custom-call(f32[2,15,2,160]{3,2,1,0:T(2,128)} %voxels_hbm.1, f32[2,2,160]{2,1,0:T(2,128)} %disparity_hbm.1, bf16[2,2,160,128]{3,2,1,0:T(8,128)(2,1)} %hidden_hbm.1, bf16[2,2,160,384]{3,2,1,0:T(8,128)(2,1)} %context_hbm.1, f32[15,256]{1,0:T(8,128)} %first_hbm.1, ...), custom_call_target="tpu_custom_call" | custom-call | tf_op jit(solution)/shard_map/pallas_call | solution.py:401
  21.4 1.6 %shard_map.141 = (bf16[2,2,160,128]{3,2,1,0:T(8,128)(2,1)}, f32[2,2,160]{2,1,0:T(2,128)}) custom-call(bf16[2,2,160,128]{3,2,1,0:T(8,128)(2,1)} %get-tuple-element.4.state_in, f32[2,2,160]{2,1,0:T(2,128)} %get-tuple-element.5.step_in), custom_call_target="tpu_custom_call" | custom-call | tf_op jit(solution)/shard_map/pallas_call | solution.py:433
